TPU v7x, 256 devices: a whole 4x4x8 slice. The times are simulated.
256 devices in a mesh: ens: 8 (over y, core), grid: 32 (over x, z).
Axes of the slice: x: 4, y: 4, z: 8, core: 2. Of those that a mesh axis runs over, the one named last changes fastest.
Arguments:
- mesh_latent: bfloat16 [8, 1024, 1024], P('ens', 'grid'), may hold values from -6 to 6
- grid_feat: bfloat16 [8, 8192, 1024], P('ens', 'grid'), may hold values from -6 to 6
- edges: int32 [8192, 3], P('grid'), may hold values from 0 to 1023, as said below
- target: float32 [8192, 100], P('grid'), may hold values from -6 to 6
- w_query: bfloat16 [1024, 1024], replicated, may hold values from -0.1875 to 0.1875
- w_key: bfloat16 [1024, 1024], replicated, may hold values from -0.1875 to 0.1875
- w_value: bfloat16 [1024, 1024], replicated, may hold values from -0.1875 to 0.1875
- w_out: bfloat16 [1024, 100], replicated, may hold values from -0.1875 to 0.1875
Outputs:
- grad_latent: float32 [8, 1024, 1024], P('ens', 'grid')
- loss: float32 [], replicated
Inputs may be any that keep to these rules, and one draw needn't show every extreme that they name: `edges`: A point of region r (points r * 256 to (r + 1) * 256 - 1) links only to mesh nodes from max(r * 32 - 8, 0) to min((r + 1) * 32 + 8, 1024) - 1, and in every region both ends of that range are linked by some point.
All inputs are finite; a program needn't handle non-finite values.
Results may differ from a plain program's by a relative error of at most 0.0096.
Values may be sent and summed in bfloat16 or wider, within the bound.
A program may use at most 64 MiB of HBM per device.

v0:
```python
import jax
import jax.numpy as jnp
from jax import lax
from jax.sharding import PartitionSpec as P

HEADS = 16
K = 3
HALO = 8


DELTA_SQ = 0.01
ALPHA = 0.95


def with_halo(cells, sides, width):
    for axis, dim in sides:
        count = lax.axis_size(axis)
        ends = count - 1
        head = lax.slice_in_dim(cells, 0, width, axis=dim)
        tail = lax.slice_in_dim(cells, cells.shape[dim] - width, cells.shape[dim], axis=dim)
        cells = jnp.concatenate(
            [
                lax.ppermute(tail, axis, [(i, (i + 1) % count) for i in range(ends)]),
                cells,
                lax.ppermute(head, axis, [((i + 1) % count, i) for i in range(ends)]),
            ],
            axis=dim,
        )
    return cells


def from_behind(value, axis, by):
    peers = lax.axis_size(axis)
    pairs = [(i, i + by) for i in range(peers) if 0 <= i + by < peers]
    return lax.ppermute(value, axis, pairs)


def smooth(x):
    return jnp.sqrt(x * x + DELTA_SQ)


def slope(x):
    return x / jnp.sqrt(x * x + DELTA_SQ)


def local(mesh_latent, grid_feat, edges, target, w_query, w_key, w_value, w_out):
    latent = mesh_latent[0]
    feats = grid_feat[0]
    own_nodes, width = latent.shape
    points = edges.shape[0]
    regions = lax.axis_size("grid")
    region = lax.axis_index("grid")
    head_size = width // HEADS
    scale = head_size ** (-0.5)
    flat_edges = edges.reshape(-1)
    local_edges = flat_edges - (region * own_nodes - HALO)
    query = jnp.dot(feats, w_query, preferred_element_type=jnp.float32).astype(jnp.bfloat16)
    keys = jnp.dot(latent, w_key, preferred_element_type=jnp.float32).astype(jnp.bfloat16)
    values = jnp.dot(latent, w_value, preferred_element_type=jnp.float32).astype(jnp.bfloat16)
    widened = with_halo(jnp.concatenate([keys, values], axis=1), (("grid", 0),), HALO)
    picked = widened[local_edges].reshape(points, K, 2 * width)
    q_heads = query.astype(jnp.float32).reshape(points, HEADS, head_size)
    k_heads = picked[..., :width].astype(jnp.float32).reshape(points, K, HEADS, head_size)
    v_heads = picked[..., width:].astype(jnp.float32).reshape(points, K, HEADS, head_size)
    scores = jnp.einsum("phd,pkhd->pkh", q_heads, k_heads) * scale
    attn = jax.nn.softmax(scores, axis=1)
    context = jnp.einsum("pkh,pkhd->phd", attn, v_heads).reshape(points, width).astype(jnp.bfloat16)
    pred = jnp.dot(context, w_out, preferred_element_type=jnp.float32)
    everyone = lax.all_gather(pred[None], "ens", axis=0, tiled=True)
    members = everyone.shape[0]
    coeff = 1.0 - (1.0 - ALPHA) / members
    spread = everyone[:, None] - everyone[None]
    local_part = jnp.sum(smooth(everyone - target[None])) / members
    local_part = local_part - coeff / (2.0 * members * (members - 1)) * jnp.sum(smooth(spread))
    total = lax.psum(local_part, "grid")
    loss = total / (points * regions * target.shape[1])
    pair_slope = jnp.sum(slope(pred[None] - everyone), axis=0)
    grad_pred = slope(pred - target) / members - coeff / (members * (members - 1)) * pair_slope
    grad_context = jnp.dot(grad_pred, w_out.T, precision=lax.Precision.HIGHEST).reshape(
        points, HEADS, head_size
    )
    grad_values = attn[..., None] * grad_context[:, None]
    grad_attn = jnp.einsum("phd,pkhd->pkh", grad_context, v_heads)
    grad_score = attn * (grad_attn - jnp.sum(attn * grad_attn, axis=1, keepdims=True))
    grad_keys = grad_score[..., None] * q_heads[:, None] * scale
    flat = jnp.concatenate([grad_keys.reshape(-1, width), grad_values.reshape(-1, width)], axis=1)
    widened_grads = (
        jnp.zeros((own_nodes + 2 * HALO, 2 * width), jnp.float32).at[local_edges].add(flat)
    )
    lower_rim = widened_grads[:HALO]
    upper_rim = widened_grads[own_nodes + HALO :]
    from_above = from_behind(lower_rim, "grid", -1)
    from_below = from_behind(upper_rim, "grid", 1)
    owned = widened_grads[HALO : own_nodes + HALO]
    owned = owned.at[:HALO].add(from_below)
    owned = owned.at[own_nodes - HALO :].add(from_above)
    mapped = jnp.dot(owned[:, :width], w_key.T, precision=lax.Precision.HIGHEST)
    grad = mapped + jnp.dot(owned[:, width:], w_value.T, precision=lax.Precision.HIGHEST)
    return (grad[None], loss)


def solution(mesh):
    in_specs = (
        P("ens", "grid", None),
        P("ens", "grid", None),
        P("grid", None),
        P("grid", None),
        P(),
        P(),
        P(),
        P(),
    )
    out_specs = (P("ens", "grid", None), P())
    return jax.shard_map(local, mesh=mesh, in_specs=in_specs, out_specs=out_specs, check_vma=False)
```

profile of v0, /device:TPU:8, one launch (start us, length us, event | category | flops | bytes accessed | tf_op | source)
XLA Modules:
  0.0 211.2 jit_solution(7226709540284002111)
XLA Ops:
  0.7 2.2 %convolution_convert_fusion.1 = bf16[32,1024]{1,0:T(8,128)(2,1)S(1)} fusion(bf16[1024,1024]{1,0:T(8,128)(2,1)} %param.18, bf16[1,32,1024]{2,1,0:T(8,128)(2,1)} %param.12), kind=kOutput, calls=%fused_computation.18 | convolution fusion | flops 67141632 | bytes 2228224 | tf_op jit(solution)/shard_map/dot_general | solution.py:59
  2.9 2.1 convolution_convert_fusion.2
  5.6 3.8 %collective-permute-start = (bf16[8,2048]{1,0:T(8,128)(2,1)}, bf16[8,2048]{1,0:T(8,128)(2,1)S(1)}, u32[]{:S(2)}, u32[]{:S(2)}) collective-permute-start(bf16[8,2048]{1,0:T(8,128)(2,1)} %get-tuple-element.32), channel_id=1, source_target_pairs={{0,1},{1,2},{2,3},{3,4},{4,5},{5,6},{6,7},{7,8},{8,9},{9,10},{10,1... | collective-permute-start | bytes 98312 | tf_op jit(solution)/shard_map/ppermute | solution.py:23
  14.1 2.5 %copy.26 = f32[256,16,64]{2,1,0:T(8,128)} copy(f32[256,16,64]{0,2,1:T(8,128)S(1)} %bitcast_convert_fusion) | data formatting | bytes 2097152 | tf_op jit(solution)/shard_map/mul | solution.py:85
  16.5 4.3 %gather_fusion = bf16[768,2048]{1,0:T(8,128)(2,1)} fusion(bf16[48,2048]{1,0:T(8,128)(2,1)S(1)} %pad_maximum_fusion, s32[1024]{0:T(1024)S(1)} %pad_clamp_fusion), kind=kCustom, calls=%fused_computation | custom fusion | bytes 6294528 | tf_op jit(solution)/shard_map/gather | solution.py:61
  20.8 9.1 %reshape.113 = bf16[256,3,2048]{2,1,0:T(4,128)(2,1)} reshape(bf16[768,2048]{1,0:T(8,128)(2,1)} %gather_fusion) | data formatting | bytes 6291456 | tf_op jit(solution)/shard_map/reshape | solution.py:61
  29.9 4.3 %fusion.41 = (bf16[256,3,1024]{2,1,0:T(4,128)(2,1)}, bf16[256,3,1024]{2,1,0:T(4,128)(2,1)}) fusion(bf16[256,3,2048]{2,1,0:T(4,128)(2,1)} %reshape.113), kind=kLoop, calls=%fused_computation.69 | loop fusion | bytes 6291456 | tf_op jit(solution)/shard_map/slice | solution.py:63
  34.3 4.1 %copy.51 = bf16[256,3,1024]{0,2,1:T(8,128)(2,1)} copy(bf16[256,3,1024]{2,1,0:T(4,128)(2,1)} %get-tuple-element.28) | data formatting | bytes 3145728
  38.4 1.9 multiply_reduce_fusion.2
  41.4 4.2 %copy.52 = bf16[256,3,1024]{0,2,1:T(8,128)(2,1)} copy(bf16[256,3,1024]{2,1,0:T(4,128)(2,1)} %get-tuple-element.29) | data formatting | bytes 3145728
  47.7 13.8 %all-gather = f32[2048,100]{0,1:T(8,128)S(1)} all-gather(f32[256,100]{0,1:T(8,128)S(1)} %fusion.45), channel_id=2, replica_groups=mesh['ens'=8,'grid'=32] {'ens'}, dimensions={0}, use_global_device_ids=true | all-gather | bytes 921600 | tf_op jit(solution)/shard_map/all_gather | solution.py:69
  65.3 2.5 %copy.27 = f32[256,16,64]{2,1,0:T(8,128)} copy(f32[256,16,64]{0,2,1:T(8,128)S(1)} %bitcast.66) | data formatting | bytes 2097152 | tf_op jit(solution)/shard_map/reshape | solution.py:79
  68.8 2.8 %fusion.9 = f32[256,3,16]{2,1,0:T(4,128)} fusion(f32[256,3,16]{2,1,0:T(4,128)} %copy-done.4, f32[256,16,3]{1,2,0:T(4,128)} %copy.50), kind=kOutput, calls=%fused_computation.26 | output fusion | flops 40962 | bytes 147456 | tf_op jit(solution)/shard_map/sub | solution.py:84
  72.9 3.8 %broadcast_multiply_fusion = f32[256,3,16,64]{3,2,1,0:T(8,128)} fusion(f32[256,16,64]{2,1,0:T(8,128)S(1)} %copy-done.2, f32[256,3,16]{2,1,0:T(4,128)S(1)} %copy-done.5), kind=kLoop, calls=%fused_computation.12 | loop fusion | flops 786432 | bytes 4243456 | tf_op jit(solution)/shard_map/mul | solution.py:82
  76.7 6.4 %mul.101 = f32[768,1024]{1,0:T(8,128)} reshape(f32[256,3,16,64]{3,2,1,0:T(8,128)} %broadcast_multiply_fusion) | data formatting | bytes 6291456 | tf_op jit(solution)/shard_map/mul | solution.py:82
  83.1 5.5 %multiply_multiply_fusion = f32[256,3,16,64]{3,2,1,0:T(8,128)} fusion(f32[256,16,64]{2,1,0:T(8,128)} %copy.26, f32[256,3,16]{2,1,0:T(4,128)S(1)} %copy-done.7), kind=kLoop, calls=%fused_computation.8 | loop fusion | flops 1572864 | bytes 4243456 | tf_op jit(solution)/shard_map/mul | solution.py:85
  88.6 6.3 %mul.97 = f32[768,1024]{1,0:T(8,128)} reshape(f32[256,3,16,64]{3,2,1,0:T(8,128)} %multiply_multiply_fusion) | data formatting | bytes 6291456 | tf_op jit(solution)/shard_map/mul | solution.py:85
  94.9 15.6 %scatter_custom_fusion = f32[48,2048]{1,0:T(8,128)S(1)} fusion(s32[768]{0:T(1024)S(1)} %fusion.35, f32[768,1024]{1,0:T(8,128)} %mul.101, f32[]{:T(128)} %constant.86.clone.1, f32[768,1024]{1,0:T(8,128)} %mul.97, f32[]{:T(128)} %constant.79.clone.1), kind=kCustom, calls=%fused_computation.4 | custom fusion | flops 3145728 | bytes 6684680 | tf_op jit(solution)/shard_map/scatter-add | solution.py:88
  110.6 4.5 %collective-permute-start.2 = (f32[8,2048]{1,0:T(8,128)S(1)}, f32[8,2048]{1,0:T(8,128)S(1)}, u32[]{:S(2)}, u32[]{:S(2)}) collective-permute-start(f32[8,2048]{1,0:T(8,128)S(1)} %get-tuple-element.31), channel_id=1, source_target_pairs={{0,1},{1,2},{2,3},{3,4},{4,5},{5,6},{6,7},{7,8},{8,9},{9,10},{10,1... | collective-permute-start | bytes 196616 | tf_op jit(solution)/shard_map/ppermute | solution.py:35
  115.1 4.1 %sqrt_reduce_fusion = f32[]{:T(128)} fusion(f32[8,256,100]{1,0,2:T(8,128)S(1)} %copy-done.3, f32[8,256,100]{1,2,0:T(8,128)} %copy.28), kind=kLoop, calls=%fused_computation.3 | loop fusion | flops 6553599 | bytes 1638404 | tf_op jit(solution)/shard_map/reduce_sum | solution.py:74
  120.5 75.6 %psum.7 = f32[]{:T(128)} all-reduce(f32[]{:T(128)S(6)} %sub.90), channel_id=1, replica_groups=mesh['ens'=8,'grid'=32] {'grid'}, use_global_device_ids=true, to_apply=%region_7.0 | all-reduce | flops 1 | bytes 8 | tf_op jit(solution)/shard_map/psum | solution.py:75
  198.4 4.0 %collective-permute-done.3 = f32[8,2048]{1,0:T(8,128)S(1)} collective-permute-done((f32[8,2048]{1,0:T(8,128)S(1)}, f32[8,2048]{1,0:T(8,128)S(1)}, u32[]{:S(2)}, u32[]{:S(2)}) %collective-permute-start.3) | collective-permute-done | bytes 65568 | tf_op jit(solution)/shard_map/ppermute | solution.py:35
  202.4 3.5 %fusion.16 = f32[32,1024]{1,0:T(8,128)S(1)} fusion(bf16[1024,1024]{1,0:T(8,128)(2,1)} %param.18, f32[32,2048]{1,0:T(8,128)S(1)} %fusion.28), kind=kOutput, calls=%fused_computation.35 | convolution fusion | flops 402653184 | bytes 2359296 | tf_op jit(solution)/shard_map/dot_general | solution.py:98
  205.9 4.2 %fusion.7 = f32[1,32,1024]{2,1,0:T(8,128)} fusion(f32[32,1024]{1,0:T(8,128)S(1)} %fusion.16, bf16[1024,1024]{1,0:T(8,128)(2,1)} %param.17, f32[32,2048]{1,0:T(8,128)S(1)} %fusion.28), kind=kOutput, calls=%fused_computation.17 | convolution fusion | flops 402685952 | bytes 2490368 | tf_op jit(solution)/shard_map/dot_general | solution.py:97
  (54 shorter events, 15.9 us)
Async XLA Ops:
  0.6 10.5 %copy-start = (bf16[1024,1024]{1,0:T(8,128)(2,1)S(1)}, bf16[1024,1024]{1,0:T(8,128)(2,1)}, u32[]{:S(2)}) copy-start(bf16[1024,1024]{1,0:T(8,128)(2,1)} %param.16) | copy-start | bytes 6291460
  0.6 10.1 %copy-start.9 = (s32[256,3]{0,1:T(4,128)S(1)}, s32[256,3]{0,1:T(4,128)}, u32[]{:S(2)}) copy-start(s32[256,3]{0,1:T(4,128)} %param.14) | copy-start | bytes 9220
  0.7 10.5 %copy-start.10 = (bf16[1,256,1024]{2,1,0:T(8,128)(2,1)S(1)}, bf16[1,256,1024]{2,1,0:T(8,128)(2,1)}, u32[]{:S(2)}) copy-start(bf16[1,256,1024]{2,1,0:T(8,128)(2,1)} %param.13) | copy-start | bytes 1572868
  5.6 10.9 %collective-permute-start = (bf16[8,2048]{1,0:T(8,128)(2,1)}, bf16[8,2048]{1,0:T(8,128)(2,1)S(1)}, u32[]{:S(2)}, u32[]{:S(2)}) collective-permute-start(bf16[8,2048]{1,0:T(8,128)(2,1)} %get-tuple-element.32), channel_id=1, source_target_pairs={{0,1},{1,2},{2,3},{3,4},{4,5},{5,6},{6,7},{7,8},{8,9},{9,10},{10,1... | collective-permute-start | bytes 98312 | tf_op jit(solution)/shard_map/ppermute | solution.py:23
  9.5 7.1 %collective-permute-start.1 = (bf16[8,2048]{1,0:T(8,128)(2,1)}, bf16[8,2048]{1,0:T(8,128)(2,1)S(1)}, u32[]{:S(2)}, u32[]{:S(2)}) collective-permute-start(bf16[8,2048]{1,0:T(8,128)(2,1)} %get-tuple-element.33), channel_id=1, source_target_pairs={{1,0},{2,1},{3,2},{4,3},{5,4},{6,5},{7,6},{8,7},{9,8},{10,9},{11,1... | collective-permute-start | bytes 98312 | tf_op jit(solution)/shard_map/ppermute | solution.py:25
  41.2 6.2 %copy-start.4 = (f32[256,3,16]{2,1,0:T(4,128)}, f32[256,3,16]{2,1,0:T(4,128)S(1)}, u32[]{:S(2)}) copy-start(f32[256,3,16]{2,1,0:T(4,128)S(1)} %fusion.14) | copy-start | bytes 147460
  41.3 6.2 %copy-start.6 = (bf16[1024,100]{0,1:T(8,128)(2,1)S(1)}, bf16[1024,100]{0,1:T(8,128)(2,1)}, u32[]{:S(2)}) copy-start(bf16[1024,100]{0,1:T(8,128)(2,1)} %param.19) | copy-start | bytes 614404
  45.6 17.2 %copy-start.8 = (f32[256,100]{0,1:T(8,128)S(1)}, f32[256,100]{0,1:T(8,128)}, u32[]{:S(2)}) copy-start(f32[256,100]{0,1:T(8,128)} %param.15) | copy-start | bytes 307204
  61.5 3.3 %copy-start.1 = (bf16[256,3,1024]{0,2,1:T(8,128)(2,1)S(1)}, bf16[256,3,1024]{0,2,1:T(8,128)(2,1)}, u32[]{:S(2)}) copy-start(bf16[256,3,1024]{0,2,1:T(8,128)(2,1)} %copy.52) | copy-start | bytes 4718596
  67.8 3.8 %copy-start.3 = (f32[8,256,100]{1,0,2:T(8,128)S(1)}, f32[8,256,100]{1,0,2:T(8,128)}, u32[]{:S(2)}) copy-start(f32[8,256,100]{1,0,2:T(8,128)} %slice_bitcast_fusion) | copy-start | bytes 2457604
  67.8 5.1 %copy-start.5 = (f32[256,3,16]{2,1,0:T(4,128)S(1)}, f32[256,3,16]{2,1,0:T(4,128)}, u32[]{:S(2)}) copy-start(f32[256,3,16]{2,1,0:T(4,128)} %copy-done.4) | copy-start | bytes 147460
  68.8 4.1 %copy-start.2 = (f32[256,16,64]{2,1,0:T(8,128)S(1)}, f32[256,16,64]{2,1,0:T(8,128)}, u32[]{:S(2)}) copy-start(f32[256,16,64]{2,1,0:T(8,128)} %copy.27) | copy-start | bytes 3145732
  76.7 6.4 %copy-start.7 = (f32[256,3,16]{2,1,0:T(4,128)S(1)}, f32[256,3,16]{2,1,0:T(4,128)}, u32[]{:S(2)}) copy-start(f32[256,3,16]{2,1,0:T(4,128)} %fusion.9) | copy-start | bytes 147460
  110.6 87.8 %collective-permute-start.2 = (f32[8,2048]{1,0:T(8,128)S(1)}, f32[8,2048]{1,0:T(8,128)S(1)}, u32[]{:S(2)}, u32[]{:S(2)}) collective-permute-start(f32[8,2048]{1,0:T(8,128)S(1)} %get-tuple-element.31), channel_id=1, source_target_pairs={{0,1},{1,2},{2,3},{3,4},{4,5},{5,6},{6,7},{7,8},{8,9},{9,10},{10,1... | collective-permute-start | bytes 196616 | tf_op jit(solution)/shard_map/ppermute | solution.py:35
  196.2 6.2 %collective-permute-start.3 = (f32[8,2048]{1,0:T(8,128)S(1)}, f32[8,2048]{1,0:T(8,128)S(1)}, u32[]{:S(2)}, u32[]{:S(2)}) collective-permute-start(f32[8,2048]{1,0:T(8,128)S(1)} %get-tuple-element.30), channel_id=1, source_target_pairs={{1,0},{2,1},{3,2},{4,3},{5,4},{6,5},{7,6},{8,7},{9,8},{10,9},{11,1... | collective-permute-start | bytes 196616 | tf_op jit(solution)/shard_map/ppermute | solution.py:35
where the time goes:
time: 212 us; the launch traced here: 211 us
  blocking collectives  89.5 us (42%)
  local copies, waits for them, and re-layouts  49 us (23%)
  other arithmetic  40 us (19%)
  matrix products  13.6 us (6%)
  starting transfers between devices  11.2 us (5%)
  between operations  4.02 us (2%)
  waiting for transfers between devices  3.97 us (2%)
    psum x1, blocking collectives, local(): total = lax.psum(local_part, 'grid')  75.6 us
    scatter-add x1, other arithmetic, local(): jnp.zeros((own_nodes + 2 * HALO, 2 * width), jnp.float32).at[local_edges]  15.6 us
    all_gather x1, blocking collectives, local(): everyone = lax.all_gather(pred[None], 'ens', axis=0, tiled=True)  13.8 us
    reshape x1, local copies, waits for them, and re-layouts, local(): picked = widened[local_edges].reshape(points, K, 2 * width)  9.1 us
    unnamed x27, local copies, waits for them, and re-layouts  9.03 us
    mul x2, local copies, waits for them, and re-layouts, local(): grad_keys = grad_score[..., None] * q_heads[:, None] * scale  8.78 us
    mul x1, local copies, waits for them, and re-layouts, local(): grad_values = attn[..., None] * grad_context[:, None]  6.38 us
    ppermute x2, starting transfers between devices, from_behind(): return lax.ppermute(value, axis, pairs)  6.06 us
  transfers between devices with their start and end apart: 4, of which 1 were waited for; matrix products, arithmetic and copies ran while one was open for 5% of the time, Pallas kernels for 0%

commit v1 on v0

v1 whole, which is shorter than its diff:
```python
import functools
import math

import jax
import jax.numpy as jnp
from jax import lax
from jax.experimental import pallas as pl
from jax.experimental.pallas import tpu as pltpu
from jax.sharding import PartitionSpec as P

HEADS = 16
HALO = 8
DELTA_SQ = 0.01
ALPHA = 0.95
LOG2E = math.log2(math.e)

MESH = pl.DeviceIdType.MESH
F32 = jnp.float32
BF16 = jnp.bfloat16

RIM = 16
ROWS = 16
GROUP = 256
NT = (((1,), (1,)), ((), ()))
TN = (((0,), (0,)), ((), ()))


def kernel(
    members, regions, deep, npts,
    latent_in, feats_in, edges_in, target_in, wq_in, wk_in, wv_in, wo_in,
    grad_out, loss_out,
    lat, feats, edges, target, wq, wk, wv, wo,
    tpad, wof, won, query, vbd, attn, attn16, pred, got, back_out, back,
    gl, halo, ens_loss, x_loss, z_loss, mine,
    load_sem, rim_send, rim_recv, go_send, go_recv, ret_send, ret_recv,
    halo_send, halo_recv, el_send, el_recv, xl_send, xl_recv, zl_send, zl_recv,
):
    me = lax.axis_index("ens")
    region = lax.axis_index("grid")
    wide = regions // deep
    rx, rz = region // deep, lax.rem(region, deep)
    own_nodes, width = latent_in.shape
    points = feats_in.shape[0]
    variables = wo_in.shape[0]
    window = own_nodes + 2 * HALO
    head_size = width // HEADS
    heads = GROUP // head_size
    groups = width // GROUP
    lower = lax.rem(region + regions - 1, regions)
    upper = lax.rem(region + 1, regions)
    peers = [lax.rem(me + k, members) for k in range(members)]
    x_peers = [lax.rem(rx + k, wide) * deep + rz for k in range(1, wide)]
    z_peers = [rx * deep + lax.rem(rz + k, deep) for k in range(1, deep)]

    def load(src, dst, k):
        copy = pltpu.make_async_copy(src, dst, load_sem.at[k])
        copy.start()
        return copy

    load_lat = load(latent_in, lat.at[pl.ds(RIM, own_nodes)], 0)
    load_feats = load(feats_in, feats, 1)
    load_wq = [
        load(wq_in.at[:, pl.ds(g * GROUP, GROUP)], wq.at[:, pl.ds(g * GROUP, GROUP)], 2 + g)
        for g in range(groups)
    ]
    load_wk = load(wk_in, wk, 6)
    load_wv = load(wv_in, wv, 7)
    load_wo = load(wo_in, wo, 8)
    load_edges = load(edges_in, edges, 9)
    load_target = load(target_in, target, 10)

    barrier = pltpu.get_barrier_semaphore()
    for k in range(1, members):
        pl.semaphore_signal(barrier, inc=1, device_id=(peers[k], region), device_id_type=MESH)
    for r in [lower, upper] + x_peers + z_peers:
        pl.semaphore_signal(barrier, inc=1, device_id=(me, r), device_id_type=MESH)
    load_lat.wait()
    pl.semaphore_wait(barrier, members - 1 + 2 + len(x_peers) + len(z_peers))

    def send(src, dst, send_sem, recv_sem, member, r):
        copy = pltpu.make_async_remote_copy(
            src_ref=src, dst_ref=dst, send_sem=send_sem, recv_sem=recv_sem,
            device_id=(member, r), device_id_type=MESH,
        )
        copy.start()
        return copy

    rims = [
        send(lat.at[pl.ds(RIM, RIM)], lat.at[pl.ds(RIM + own_nodes, RIM)],
             rim_send.at[0], rim_recv.at[0], me, lower),
        send(lat.at[pl.ds(own_nodes, RIM)], lat.at[pl.ds(0, RIM)],
             rim_send.at[1], rim_recv.at[1], me, upper),
    ]

    load_feats.wait()
    for g in range(groups):
        cols = pl.ds(g * GROUP, GROUP)
        load_wq[g].wait()
        query[:, cols] = jnp.dot(
            feats[...], wq[:, cols], preferred_element_type=F32
        ).astype(BF16)

    load_edges.wait()
    links = edges[...] - (region * own_nodes - HALO)
    node = lax.broadcasted_iota(jnp.int32, (window, points), 0)
    count = jnp.zeros((window, points), F32)
    for e in range(edges_in.shape[0]):
        count = count + jnp.where(node == links[e : e + 1, :], 1.0, 0.0)
    linked = count > 0.0
    head_of = lax.broadcasted_iota(jnp.int32, (window, GROUP), 1) // head_size

    def spread(x):
        return jnp.concatenate(
            [jnp.where(head_of == h, x, 0.0) for h in range(heads)], axis=0
        ).astype(BF16)

    def gather(x):
        out = jnp.zeros((window, GROUP), F32)
        for h in range(heads):
            out = jnp.where(head_of == h, x[h * window : (h + 1) * window], out)
        return out

    load_wo.wait()
    load_wk.wait()
    load_wv.wait()
    for rim in rims:
        rim.wait()
    total = jnp.zeros((variables, points), F32)
    scale = head_size ** (-0.5)
    for g in range(groups):
        cols = pl.ds(g * GROUP, GROUP)
        keys = jnp.dot(lat[...], wk[:, cols], preferred_element_type=F32)
        values = jnp.dot(lat[...], wv[:, cols], preferred_element_type=F32)
        kb = spread(keys[RIM - HALO : RIM - HALO + window])
        vb = spread(values[RIM - HALO : RIM - HALO + window])
        vbd[g] = vb
        scores = lax.dot_general(kb, query[:, cols], NT, preferred_element_type=F32)
        for h in range(heads):
            rows = pl.ds(h * window, window)
            s = jnp.where(linked, scores[h * window : (h + 1) * window], -jnp.inf)
            top = jnp.max(s, axis=0, keepdims=True)
            e = count * jnp.exp2((s - top) * (scale * LOG2E))
            a = e * (1.0 / jnp.sum(e, axis=0, keepdims=True))
            attn[g, rows, :] = a
        a16 = attn[g].astype(BF16)
        attn16[g] = a16
        ctx = lax.dot_general(vb, a16, TN, preferred_element_type=F32).astype(BF16)
        total = total + jnp.dot(wo[:, cols], ctx, preferred_element_type=F32)
    pred[...] = jnp.zeros_like(pred)
    pred[pl.ds(0, variables), :] = total

    gone = [
        send(pred.at[pl.ds(pl.multiple_of(peers[k] * ROWS, ROWS), ROWS)], got.at[k],
             go_send.at[k], go_recv.at[k], peers[k], region)
        for k in range(1, members)
    ]
    load_target.wait()
    tpad[...] = jnp.zeros_like(tpad)
    tpad[pl.ds(0, variables), :] = target[...]
    wof[...] = jnp.zeros_like(wof)
    wof[pl.ds(0, variables), :] = wo[...].astype(F32)
    won[...] = wof[...].T.astype(BF16)

    first = pl.multiple_of(me * ROWS, ROWS)
    got[0] = pred[pl.ds(first, ROWS), :]
    for copy in gone:
        copy.wait()

    coeff = 1.0 - (1.0 - ALPHA) / members
    pair = coeff / (members * (members - 1))
    loss_part = jnp.zeros((8, 128), F32)
    for top in range(0, ROWS, 8):
        row = lax.broadcasted_iota(jnp.int32, (8, 128), 0) + first + top
        valid = row < variables
        block_loss = jnp.zeros((8, 128), F32)
        for left in range(0, points, 128):
            at = (pl.ds(top, 8), pl.ds(left, 128))
            goal = tpad[pl.ds(first + top, 8), pl.ds(left, 128)]
            ps = [got[(k,) + at] for k in range(members)]
            slopes = [None] * members
            near = jnp.zeros((8, 128), F32)
            apart = jnp.full((8, 128), 0.5 * members * math.sqrt(DELTA_SQ), F32)
            grads = []
            for i in range(members):
                d = ps[i] - goal
                sq = d * d + DELTA_SQ
                inv = lax.rsqrt(sq)
                near = near + sq * inv
                grads.append(d * inv)
            for i in range(members):
                for j in range(i + 1, members):
                    d = ps[i] - ps[j]
                    sq = d * d + DELTA_SQ
                    inv = lax.rsqrt(sq)
                    apart = apart + sq * inv
                    d = d * inv
                    slopes[i] = d if slopes[i] is None else slopes[i] + d
                    slopes[j] = -d if slopes[j] is None else slopes[j] - d
            block_loss = block_loss + (near * (1.0 / members) - apart * pair)
            for i in range(members):
                back_out[(i,) + at] = (grads[i] * (1.0 / members) - slopes[i] * pair).astype(BF16)
        loss_part = loss_part + jnp.where(valid, block_loss, 0.0)

    returned = []
    for k in range(1, members):
        owner = lax.rem(me + members - k, members)
        returned.append(
            send(back_out.at[k], back.at[pl.ds(first, ROWS)],
                 ret_send.at[k], ret_recv.at[k], owner, region)
        )
    mine[0] = loss_part
    ens_loss[me] = loss_part
    el = [
        send(mine.at[0], ens_loss.at[me], el_send.at[k], el_recv.at[k], peers[k], region)
        for k in range(1, members)
    ]
    back[pl.ds(first, ROWS), :] = back_out[0]
    for copy in returned:
        copy.wait()

    for copy in el:
        copy.wait()
    loss_part = ens_loss[0]
    for k in range(1, members):
        loss_part = loss_part + ens_loss[k]
    mine[1] = loss_part
    x_loss[rx] = loss_part
    xl = [
        send(mine.at[1], x_loss.at[rx], xl_send.at[k], xl_recv.at[k], me, r)
        for k, r in enumerate(x_peers)
    ]

    gk, gv = [], []
    for g in range(groups):
        cols = pl.ds(g * GROUP, GROUP)
        gc = jnp.dot(won[cols, :], back[...], preferred_element_type=F32).astype(BF16)
        ga = jnp.dot(vbd[g], gc, preferred_element_type=F32)
        parts = []
        for h in range(heads):
            a = attn[g, pl.ds(h * window, window), :]
            t = a * ga[h * window : (h + 1) * window]
            parts.append(t - a * jnp.sum(t, axis=0, keepdims=True))
        gs = jnp.concatenate(parts, axis=0).astype(BF16)
        gk.append((gather(jnp.dot(gs, query[:, cols], preferred_element_type=F32)) * scale).astype(BF16))
        gv.append(gather(lax.dot_general(attn16[g], gc, NT, preferred_element_type=F32)).astype(BF16))
    gk = jnp.concatenate(gk, axis=1)
    gv = jnp.concatenate(gv, axis=1)

    for copy in xl:
        copy.wait()
    loss_part = x_loss[0]
    for k in range(1, wide):
        loss_part = loss_part + x_loss[k]
    mine[2] = loss_part
    z_loss[rz] = loss_part
    zl = [
        send(mine.at[2], z_loss.at[rz], zl_send.at[k], zl_recv.at[k], me, r)
        for k, r in enumerate(z_peers)
    ]

    for c in range(width // GROUP):
        cols = pl.ds(c * GROUP, GROUP)
        out = lax.dot_general(gk, wk[cols, :], NT, preferred_element_type=F32)
        gl[:, cols] = out + lax.dot_general(gv, wv[cols, :], NT, preferred_element_type=F32)
    rims = [
        send(gl.at[pl.ds(0, HALO)], halo.at[1], halo_send.at[0], halo_recv.at[0], me, lower),
        send(gl.at[pl.ds(window - HALO, HALO)], halo.at[0], halo_send.at[1], halo_recv.at[1], me, upper),
    ]
    grad_out[pl.ds(HALO, own_nodes - 2 * HALO), :] = gl[pl.ds(2 * HALO, own_nodes - 2 * HALO), :]

    for copy in zl:
        copy.wait()
    loss_part = z_loss[0]
    for k in range(1, deep):
        loss_part = loss_part + z_loss[k]
    loss_out[...] = jnp.sum(loss_part, keepdims=True) * (1.0 / npts)

    for rim in rims:
        rim.wait()
    grad_out[pl.ds(0, HALO), :] = gl[pl.ds(HALO, HALO), :] + halo[0]
    grad_out[pl.ds(own_nodes - HALO, HALO), :] = gl[pl.ds(own_nodes, HALO), :] + halo[1]


def local(members, regions, mesh_latent, grid_feat, edges, target, w_query, w_key, w_value, w_out):
    latent = mesh_latent[0]
    feats = grid_feat[0]
    own_nodes, width = latent.shape
    points, links = edges.shape
    variables = target.shape[1]
    window = own_nodes + 2 * HALO
    deep = math.gcd(regions, 8) if regions > 8 else 2
    wide = regions // deep
    groups = width // GROUP
    stack = window * GROUP // (width // HEADS)
    padded = members * ROWS
    dma = pltpu.SemaphoreType.DMA
    any_space = pl.BlockSpec(memory_space=pltpu.HBM)
    vmem = pl.BlockSpec(memory_space=pltpu.VMEM)
    grad, loss = pl.pallas_call(
        functools.partial(kernel, members, regions, deep, points * regions * variables),
        out_shape=(
            jax.ShapeDtypeStruct((own_nodes, width), F32),
            jax.ShapeDtypeStruct((1, 1), F32),
        ),
        in_specs=[any_space] * 8,
        out_specs=(vmem, vmem),
        scratch_shapes=[
            pltpu.VMEM((own_nodes + 2 * RIM, width), BF16),
            pltpu.VMEM((points, width), BF16),
            pltpu.VMEM((links, points), jnp.int32),
            pltpu.VMEM((variables, points), F32),
            pltpu.VMEM((width, width), BF16),
            pltpu.VMEM((width, width), BF16),
            pltpu.VMEM((width, width), BF16),
            pltpu.VMEM((variables, width), BF16),
            pltpu.VMEM((padded, points), F32),
            pltpu.VMEM((padded, width), F32),
            pltpu.VMEM((width, padded), BF16),
            pltpu.VMEM((points, width), BF16),
            pltpu.VMEM((groups, stack, GROUP), BF16),
            pltpu.VMEM((groups, stack, points), F32),
            pltpu.VMEM((groups, stack, points), BF16),
            pltpu.VMEM((padded, points), F32),
            pltpu.VMEM((members, ROWS, points), F32),
            pltpu.VMEM((members, ROWS, points), BF16),
            pltpu.VMEM((padded, points), BF16),
            pltpu.VMEM((window, width), F32),
            pltpu.VMEM((2, HALO, width), F32),
            pltpu.VMEM((members, 8, 128), F32),
            pltpu.VMEM((wide, 8, 128), F32),
            pltpu.VMEM((deep, 8, 128), F32),
            pltpu.VMEM((3, 8, 128), F32),
            dma((11,)),
            dma((2,)), dma((2,)),
            dma((members,)), dma((members,)),
            dma((members,)), dma((members,)),
            dma((2,)), dma((2,)),
            dma((members,)), dma((members,)),
            dma((wide,)), dma((wide,)),
            dma((deep,)), dma((deep,)),
        ],
        compiler_params=pltpu.CompilerParams(
            collective_id=0, has_side_effects=True, vmem_limit_bytes=48 * 1024 * 1024
        ),
    )(latent, feats, edges.T, target.T, w_query, w_key, w_value, w_out.T)
    return grad[None], loss[0, 0]


def solution(mesh):
    in_specs = (
        P("ens", "grid", None),
        P("ens", "grid", None),
        P("grid", None),
        P("grid", None),
        P(),
        P(),
        P(),
        P(),
    )
    out_specs = (P("ens", "grid", None), P())
    return jax.shard_map(
        functools.partial(local, mesh.shape["ens"], mesh.shape["grid"]),
        mesh=mesh, in_specs=in_specs, out_specs=out_specs, check_vma=False,
    )
```

time: 212 us -> 45.9 us (0.22)
  the two profiles are of different devices: /device:TPU:8 before, /device:TPU:1 now
where the time goes in v1:
time: 45.9 us; the launch traced here: 45.6 us
  Pallas kernels  35 us (76%)
  local copies, waits for them, and re-layouts  8.23 us (18%)
  between operations  2.34 us (5%)
    pallas_call x1, Pallas kernels, local(): pl.pallas_call(functools.partial(kernel, members, regions, deep, points *...  35 us
    unnamed x15, local copies, waits for them, and re-layouts  8.23 us

profile of v1, /device:TPU:1, one launch (start us, length us, event | category | flops | bytes accessed | tf_op | source)
XLA Modules:
  0.0 45.6 jit_solution(12178911437515105574)
XLA Ops:
  0.6 0.0 copy-start
  0.6 1.6 %copy-done = bf16[1024,1024]{1,0:T(8,128)(2,1)S(1)} copy-done((bf16[1024,1024]{1,0:T(8,128)(2,1)S(1)}, bf16[1024,1024]{1,0:T(8,128)(2,1)}, u32[]{:S(2)}) %copy-start) | copy-done | bytes 2097176
  2.2 0.0 copy-start.1
  2.2 1.6 %copy-done.1 = bf16[1024,1024]{1,0:T(8,128)(2,1)S(1)} copy-done((bf16[1024,1024]{1,0:T(8,128)(2,1)S(1)}, bf16[1024,1024]{1,0:T(8,128)(2,1)}, u32[]{:S(2)}) %copy-start.1) | copy-done | bytes 2097176
  3.8 0.0 copy-start.2
  3.8 1.0 %copy-done.2 = bf16[1,256,1024]{2,1,0:T(8,128)(2,1)S(1)} copy-done((bf16[1,256,1024]{2,1,0:T(8,128)(2,1)S(1)}, bf16[1,256,1024]{2,1,0:T(8,128)(2,1)}, u32[]{:S(2)}) %copy-start.2) | copy-done | bytes 524312
  4.9 0.0 copy-start.3
  4.9 0.9 %copy-done.3 = bf16[1024,100]{0,1:T(8,128)(2,1)S(1)} copy-done((bf16[1024,100]{0,1:T(8,128)(2,1)S(1)}, bf16[1024,100]{0,1:T(8,128)(2,1)}, u32[]{:S(2)}) %copy-start.3) | copy-done | bytes 204824
  5.8 0.0 copy-start.4
  5.8 0.9 %copy-done.4 = f32[256,100]{0,1:T(8,128)S(1)} copy-done((f32[256,100]{0,1:T(8,128)S(1)}, f32[256,100]{0,1:T(8,128)}, u32[]{:S(2)}) %copy-start.4) | copy-done | bytes 102424
  6.7 0.0 copy-start.5
  6.7 0.8 %copy-done.5 = bf16[1,32,1024]{2,1,0:T(8,128)(2,1)S(1)} copy-done((bf16[1,32,1024]{2,1,0:T(8,128)(2,1)S(1)}, bf16[1,32,1024]{2,1,0:T(8,128)(2,1)}, u32[]{:S(2)}) %copy-start.5) | copy-done | bytes 65560
  7.5 0.0 copy-start.6
  7.5 0.7 %copy-done.6 = s32[256,3]{0,1:T(4,128)S(1)} copy-done((s32[256,3]{0,1:T(4,128)S(1)}, s32[256,3]{0,1:T(4,128)}, u32[]{:S(2)}) %copy-start.6) | copy-done | bytes 3096
  8.2 35.0 %shard_map.95 = (f32[32,1024]{1,0:T(8,128)S(1)}, f32[1,1]{1,0:T(1,128)}) custom-call(bf16[32,1024]{1,0:T(8,128)(2,1)S(1)} %bitcast.11, bf16[256,1024]{1,0:T(8,128)(2,1)S(1)} %bitcast.7, s32[3,256]{1,0:T(4,128)S(1)} %bitcast.12, f32[100,256]{1,0:T(8,128)S(1)} %bitcast.10, bf16[1024,1024]{1,0:T(8,128)(2,1)S(1)} %copy-done, bf16[1024,1024]{1,0:T(8,128)(2,1)S(1)} %copy-done.1, ...), custom_call_target="tpu_custom_call" | custom-call | tf_op jit(solution)/shard_map/pallas_call | solution.py:299
  43.2 0.7 %copy.12 = f32[1,32,1024]{2,1,0:T(8,128)} copy(f32[1,32,1024]{2,1,0:T(8,128)S(1)} %bitcast.9) | data formatting | bytes 262144
Async XLA Ops:
  0.6 1.6 %copy-start = (bf16[1024,1024]{1,0:T(8,128)(2,1)S(1)}, bf16[1024,1024]{1,0:T(8,128)(2,1)}, u32[]{:S(2)}) copy-start(bf16[1024,1024]{1,0:T(8,128)(2,1)} %wq_in.1) | copy-start | bytes 6291460
  2.2 1.6 %copy-start.1 = (bf16[1024,1024]{1,0:T(8,128)(2,1)S(1)}, bf16[1024,1024]{1,0:T(8,128)(2,1)}, u32[]{:S(2)}) copy-start(bf16[1024,1024]{1,0:T(8,128)(2,1)} %wk_in.1) | copy-start | bytes 6291460
  3.8 1.0 %copy-start.2 = (bf16[1,256,1024]{2,1,0:T(8,128)(2,1)S(1)}, bf16[1,256,1024]{2,1,0:T(8,128)(2,1)}, u32[]{:S(2)}) copy-start(bf16[1,256,1024]{2,1,0:T(8,128)(2,1)} %param.9) | copy-start | bytes 1572868
  4.9 0.9 %copy-start.3 = (bf16[1024,100]{0,1:T(8,128)(2,1)S(1)}, bf16[1024,100]{0,1:T(8,128)(2,1)}, u32[]{:S(2)}) copy-start(bf16[1024,100]{0,1:T(8,128)(2,1)} %param.15) | copy-start | bytes 614404
  5.8 0.9 %copy-start.4 = (f32[256,100]{0,1:T(8,128)S(1)}, f32[256,100]{0,1:T(8,128)}, u32[]{:S(2)}) copy-start(f32[256,100]{0,1:T(8,128)} %param.11) | copy-start | bytes 307204
  6.7 0.8 %copy-start.5 = (bf16[1,32,1024]{2,1,0:T(8,128)(2,1)S(1)}, bf16[1,32,1024]{2,1,0:T(8,128)(2,1)}, u32[]{:S(2)}) copy-start(bf16[1,32,1024]{2,1,0:T(8,128)(2,1)} %param.8) | copy-start | bytes 196612
  7.5 0.7 %copy-start.6 = (s32[256,3]{0,1:T(4,128)S(1)}, s32[256,3]{0,1:T(4,128)}, u32[]{:S(2)}) copy-start(s32[256,3]{0,1:T(4,128)} %param.10) | copy-start | bytes 9220

commit v2 on v1

v2 whole, which is shorter than its diff:
```python
import functools
import math

import jax
import jax.numpy as jnp
from jax import lax
from jax.experimental import pallas as pl
from jax.experimental.pallas import tpu as pltpu
from jax.sharding import PartitionSpec as P

HEADS = 16
HALO = 8
DELTA_SQ = 0.01
ALPHA = 0.95
LOG2E = math.log2(math.e)

MESH = pl.DeviceIdType.MESH
F32 = jnp.float32
BF16 = jnp.bfloat16

CORES = 2
ROWS = 16
GROUP = 256
NT = (((1,), (1,)), ((), ()))
TN = (((0,), (0,)), ((), ()))


def kernel(
    members, regions, deep, npts,
    latent_in, feats_in, edges_in, target_in, wq_in, wk_in, wv_in, wo_in,
    grad_out, loss_out,
    lat, feats, edges, target, wq, wk, wv, wo,
    kv, rim_out, rim_in, tpad, wof, won, query, kbd, vbd, attn, attn16, pred, got, back_out, back,
    gl, halo, plane_loss, deep_loss, mine,
    hello, load_sem, rim_send, rim_recv, go_send, go_recv, ret_send, ret_recv,
    halo_send, halo_recv, pl_send, pl_recv, dl_send, dl_recv,
):
    me = lax.axis_index("ens")
    region = lax.axis_index("grid")
    wide, tall = regions // deep, members // CORES
    rx, rz = region // deep, lax.rem(region, deep)
    ry, rc = me // CORES, lax.rem(me, CORES)
    own_nodes, width = latent_in.shape
    points = feats_in.shape[0]
    variables = wo_in.shape[0]
    window = own_nodes + 2 * HALO
    head_size = width // HEADS
    heads = GROUP // head_size
    groups = width // GROUP
    lower = lax.rem(region + regions - 1, regions)
    upper = lax.rem(region + 1, regions)
    peers = [lax.rem(me + k, members) for k in range(members)]
    plane, line = [], []
    for i in range(1, wide * tall):
        x, y = lax.rem(rx + i // tall, wide), lax.rem(ry + i % tall, tall)
        plane.append((i // tall, y * CORES + rc, x * deep + rz))
    for i in range(1, deep * CORES):
        z, c = lax.rem(rz + i // CORES, deep), lax.rem(rc + i % CORES, CORES)
        line.append((i // CORES, ry * CORES + c, rx * deep + z))

    def load(src, dst, k):
        copy = pltpu.make_async_copy(src, dst, load_sem.at[k])
        copy.start()
        return copy

    def load_columns(src, dst, k):
        return [
            load(src.at[:, pl.ds(g * GROUP, GROUP)], dst.at[:, pl.ds(g * GROUP, GROUP)], k + g)
            for g in range(groups)
        ]

    barrier = pltpu.get_barrier_semaphore()
    near = [
        (ry * CORES + c, rx * deep + lax.rem(rz + step, deep)) for step in (1, deep - 1, 2, deep - 2) for c in range(CORES)
    ]
    greet = [(me, lower), (me, upper)] + near + [(peers[k], region) for k in range(1, members)]
    greet += [(me, lax.rem(rx + k, wide) * deep + rz) for k in range(1, wide)]
    for device in greet:
        pl.semaphore_signal(barrier, inc=1, device_id=device, device_id_type=MESH)

    load_lat = load(latent_in, lat, 0)
    load_wk = load_columns(wk_in, wk, 1)
    load_wv = load_columns(wv_in, wv, 5)
    load_feats = load(feats_in, feats, 9)
    load_wq = load_columns(wq_in, wq, 10)
    load_edges = load(edges_in, edges, 14)
    load_wo = load(wo_in, wo, 15)
    load_target = load(target_in, target, 16)

    def send(src, dst, send_sem, recv_sem, member, r):
        copy = pltpu.make_async_remote_copy(
            src_ref=src, dst_ref=dst, send_sem=send_sem, recv_sem=recv_sem,
            device_id=(member, r), device_id_type=MESH,
        )
        copy.start()
        return copy

    load_lat.wait()
    for g in range(groups):
        cols = pl.ds(g * GROUP, GROUP)
        for i, (loads, w) in enumerate(((load_wk, wk), (load_wv, wv))):
            loads[g].wait()
            kv[i, :, cols] = jnp.dot(lat[...], w[:, cols], preferred_element_type=F32)
    for side, row in enumerate((0, own_nodes - HALO)):
        rim_out[side] = jnp.concatenate(
            [kv[0, pl.ds(row, HALO), :], kv[1, pl.ds(row, HALO), :]], axis=0
        ).astype(BF16)
    pl.semaphore_wait(barrier, len(greet))
    rims = [
        send(rim_out.at[0], rim_in.at[1], rim_send.at[0], rim_recv.at[0], me, lower),
        send(rim_out.at[1], rim_in.at[0], rim_send.at[1], rim_recv.at[1], me, upper),
    ]
    for device in near[len(near) // 2 :]:
        pl.semaphore_signal(hello, inc=1, device_id=device, device_id_type=MESH)

    load_feats.wait()
    for g in range(groups):
        cols = pl.ds(g * GROUP, GROUP)
        load_wq[g].wait()
        query[:, cols] = jnp.dot(
            feats[...], wq[:, cols], preferred_element_type=F32
        ).astype(BF16)

    load_edges.wait()
    links = edges[...] - region * own_nodes
    links = jnp.where(links < 0, links + window, links)
    node = lax.broadcasted_iota(jnp.int32, (window, points), 0)
    node = jnp.where(node < own_nodes, node, jnp.where(node < own_nodes + HALO, node + HALO, node - HALO))
    count = jnp.zeros((window, points), F32)
    for e in range(edges_in.shape[0]):
        count = count + jnp.where(node == links[e : e + 1, :], 1.0, 0.0)
    linked = count > 0.0

    def head_of(rows):
        return lax.broadcasted_iota(jnp.int32, (rows, GROUP), 1) // head_size

    def spread(x, h):
        return jnp.where(head_of(x.shape[0]) == h, x, 0.0).astype(BF16)

    def gather(x):
        out = jnp.zeros((window, GROUP), F32)
        for h in range(heads):
            out = jnp.where(head_of(window) == h, x[h * window : (h + 1) * window], out)
        return out

    for g in range(groups):
        for h in range(heads):
            for i, dst in enumerate((kbd, vbd)):
                dst[g, pl.ds(h * window, own_nodes), :] = spread(kv[i, :, pl.ds(g * GROUP, GROUP)], h)

    load_target.wait()
    load_wo.wait()
    tpad[...] = jnp.zeros_like(tpad)
    tpad[pl.ds(0, variables), :] = target[...]
    wof[...] = jnp.zeros_like(wof)
    wof[pl.ds(0, variables), :] = wo[...].astype(F32)
    won[...] = wof[...].T.astype(BF16)
    pred[...] = jnp.zeros_like(pred)

    for rim in rims:
        rim.wait()
    for i, dst in enumerate((kbd, vbd)):
        for g in range(groups):
            cols = pl.ds(g * GROUP, GROUP)
            both = jnp.concatenate(
                [rim_in[side, :, cols].astype(F32)[i * HALO : (i + 1) * HALO] for side in range(2)], axis=0
            )
            for h in range(heads):
                dst[g, pl.ds(h * window + own_nodes, 2 * HALO), :] = spread(both, h)
    total = jnp.zeros((variables, points), F32)
    scale = head_size ** (-0.5)
    for g in range(groups):
        cols = pl.ds(g * GROUP, GROUP)
        scores = lax.dot_general(kbd[g], query[:, cols], NT, preferred_element_type=F32)
        parts = []
        for h in range(heads):
            s = jnp.where(linked, scores[h * window : (h + 1) * window], -jnp.inf)
            top = jnp.max(s, axis=0, keepdims=True)
            e = count * jnp.exp2((s - top) * (scale * LOG2E))
            a = e * (1.0 / jnp.sum(e, axis=0, keepdims=True))
            attn[g, pl.ds(h * window, window), :] = a
            parts.append(a.astype(BF16))
        a16 = jnp.concatenate(parts, axis=0)
        attn16[g] = a16
        ctx = lax.dot_general(vbd[g], a16, TN, preferred_element_type=F32).astype(BF16)
        total = total + jnp.dot(wo[:, cols], ctx, preferred_element_type=F32)
    pred[pl.ds(0, variables), :] = total

    gone = [
        send(pred.at[pl.ds(pl.multiple_of(peers[k] * ROWS, ROWS), ROWS)], got.at[k],
             go_send.at[k], go_recv.at[k], peers[k], region)
        for k in range(1, members)
    ]
    first = pl.multiple_of(me * ROWS, ROWS)
    got[0] = pred[pl.ds(first, ROWS), :]
    for copy in gone:
        copy.wait()

    coeff = 1.0 - (1.0 - ALPHA) / members
    pair = coeff / (members * (members - 1))
    loss_part = jnp.zeros((8, 128), F32)
    for top in range(0, ROWS, 8):
        row = lax.broadcasted_iota(jnp.int32, (8, 128), 0) + first + top
        valid = row < variables
        block_loss = jnp.zeros((8, 128), F32)
        for left in range(0, points, 128):
            at = (pl.ds(top, 8), pl.ds(left, 128))
            goal = tpad[pl.ds(first + top, 8), pl.ds(left, 128)]
            ps = [got[(k,) + at] for k in range(members)]
            slopes = [None] * members
            near = jnp.zeros((8, 128), F32)
            apart = jnp.full((8, 128), 0.5 * members * math.sqrt(DELTA_SQ), F32)
            grads = []
            for i in range(members):
                d = ps[i] - goal
                sq = d * d + DELTA_SQ
                inv = lax.rsqrt(sq)
                near = near + sq * inv
                grads.append(d * inv)
            for i in range(members):
                for j in range(i + 1, members):
                    d = ps[i] - ps[j]
                    sq = d * d + DELTA_SQ
                    inv = lax.rsqrt(sq)
                    apart = apart + sq * inv
                    d = d * inv
                    slopes[i] = d if slopes[i] is None else slopes[i] + d
                    slopes[j] = -d if slopes[j] is None else slopes[j] - d
            block_loss = block_loss + (near * (1.0 / members) - apart * pair)
            for i in range(members):
                back_out[(i,) + at] = (grads[i] * (1.0 / members) - slopes[i] * pair).astype(BF16)
        loss_part = loss_part + jnp.where(valid, block_loss, 0.0)

    loss_part = jnp.sum(loss_part, axis=0, keepdims=True)
    mine[0] = loss_part
    slot = rx * tall + ry
    plane_loss[slot] = loss_part
    plane_sent = [
        send(mine.at[0], plane_loss.at[slot], pl_send.at[k], pl_recv.at[k], m, r)
        for k, (_, m, r) in enumerate(plane)
    ]
    returned = []
    for k in range(1, members):
        owner = lax.rem(me + members - k, members)
        returned.append(
            send(back_out.at[k], back.at[pl.ds(first, ROWS)],
                 ret_send.at[k], ret_recv.at[k], owner, region)
        )
    back[pl.ds(first, ROWS), :] = back_out[0]
    for copy in returned:
        copy.wait()

    gk, gv = [], []
    for g in range(groups):
        cols = pl.ds(g * GROUP, GROUP)
        gc = jnp.dot(won[cols, :], back[...], preferred_element_type=F32).astype(BF16)
        ga = jnp.dot(vbd[g], gc, preferred_element_type=F32)
        parts = []
        for h in range(heads):
            a = attn[g, pl.ds(h * window, window), :]
            t = a * ga[h * window : (h + 1) * window]
            parts.append(t - a * jnp.sum(t, axis=0, keepdims=True))
        gs = jnp.concatenate(parts, axis=0).astype(BF16)
        gk.append((gather(jnp.dot(gs, query[:, cols], preferred_element_type=F32)) * scale).astype(BF16))
        gv.append(gather(lax.dot_general(attn16[g], gc, NT, preferred_element_type=F32)).astype(BF16))
        if g == 1:
            pl.semaphore_wait(hello, len(near) // 2)
            for copy in plane_sent:
                copy.wait()
            loss_part = plane_loss[0]
            for k in range(1, wide * tall):
                loss_part = loss_part + plane_loss[k]
            mine[1] = loss_part
            slot = rz * CORES + rc
            deep_loss[slot] = loss_part
            line_sent = [
                send(mine.at[1], deep_loss.at[slot], dl_send.at[k], dl_recv.at[k], m, r)
                for k, (_, m, r) in enumerate(line)
            ]
    gk = jnp.concatenate(gk, axis=1)
    gv = jnp.concatenate(gv, axis=1)

    for c in range(width // GROUP):
        cols = pl.ds(c * GROUP, GROUP)
        out = lax.dot_general(gk, wk[cols, :], NT, preferred_element_type=F32)
        gl[:, cols] = out + lax.dot_general(gv, wv[cols, :], NT, preferred_element_type=F32)
    rims = [
        send(gl.at[pl.ds(own_nodes, HALO)], halo.at[1], halo_send.at[0], halo_recv.at[0], me, lower),
        send(gl.at[pl.ds(own_nodes + HALO, HALO)], halo.at[0], halo_send.at[1], halo_recv.at[1], me, upper),
    ]
    grad_out[pl.ds(HALO, own_nodes - 2 * HALO), :] = gl[pl.ds(HALO, own_nodes - 2 * HALO), :]

    for rim in rims:
        rim.wait()
    grad_out[pl.ds(0, HALO), :] = gl[pl.ds(0, HALO), :] + halo[0]
    grad_out[pl.ds(own_nodes - HALO, HALO), :] = gl[pl.ds(own_nodes - HALO, HALO), :] + halo[1]

    for copy in line_sent:
        copy.wait()
    loss_part = deep_loss[0]
    for k in range(1, deep * CORES):
        loss_part = loss_part + deep_loss[k]
    loss_out[...] = jnp.sum(loss_part, keepdims=True) * (1.0 / npts)


def local(members, regions, mesh_latent, grid_feat, edges, target, w_query, w_key, w_value, w_out):
    latent = mesh_latent[0]
    feats = grid_feat[0]
    own_nodes, width = latent.shape
    points, links = edges.shape
    variables = target.shape[1]
    window = own_nodes + 2 * HALO
    deep = math.gcd(regions, 8) if regions > 8 else 2
    wide, tall = regions // deep, members // CORES
    groups = width // GROUP
    stack = window * GROUP // (width // HEADS)
    padded = members * ROWS
    dma = pltpu.SemaphoreType.DMA
    any_space = pl.BlockSpec(memory_space=pltpu.HBM)
    vmem = pl.BlockSpec(memory_space=pltpu.VMEM)
    grad, loss = pl.pallas_call(
        functools.partial(kernel, members, regions, deep, points * regions * variables),
        out_shape=(
            jax.ShapeDtypeStruct((own_nodes, width), F32),
            jax.ShapeDtypeStruct((1, 1), F32),
        ),
        in_specs=[any_space] * 8,
        out_specs=(vmem, vmem),
        scratch_shapes=[
            pltpu.VMEM((own_nodes, width), BF16),
            pltpu.VMEM((points, width), BF16),
            pltpu.VMEM((links, points), jnp.int32),
            pltpu.VMEM((variables, points), F32),
            pltpu.VMEM((width, width), BF16),
            pltpu.VMEM((width, width), BF16),
            pltpu.VMEM((width, width), BF16),
            pltpu.VMEM((variables, width), BF16),
            pltpu.VMEM((2, own_nodes, width), F32),
            pltpu.VMEM((2, 2 * HALO, width), BF16),
            pltpu.VMEM((2, 2 * HALO, width), BF16),
            pltpu.VMEM((padded, points), F32),
            pltpu.VMEM((padded, width), F32),
            pltpu.VMEM((width, padded), BF16),
            pltpu.VMEM((points, width), BF16),
            pltpu.VMEM((groups, stack, GROUP), BF16),
            pltpu.VMEM((groups, stack, GROUP), BF16),
            pltpu.VMEM((groups, stack, points), F32),
            pltpu.VMEM((groups, stack, points), BF16),
            pltpu.VMEM((padded, points), F32),
            pltpu.VMEM((members, ROWS, points), F32),
            pltpu.VMEM((members, ROWS, points), BF16),
            pltpu.VMEM((padded, points), BF16),
            pltpu.VMEM((window, width), F32),
            pltpu.VMEM((2, HALO, width), F32),
            pltpu.VMEM((wide * tall, 1, 128), F32),
            pltpu.VMEM((deep * CORES, 1, 128), F32),
            pltpu.VMEM((2, 1, 128), F32),
            pltpu.SemaphoreType.REGULAR,
            dma((17,)),
            dma((2,)), dma((2,)),
            dma((members,)), dma((members,)),
            dma((members,)), dma((members,)),
            dma((2,)), dma((2,)),
            dma((wide * tall,)), dma((wide * tall,)),
            dma((deep * CORES,)), dma((deep * CORES,)),
        ],
        compiler_params=pltpu.CompilerParams(
            collective_id=0, has_side_effects=True, vmem_limit_bytes=24 * 1024 * 1024
        ),
    )(*[pltpu.with_memory_space_constraint(x, pltpu.HBM) for x in (latent, feats, edges.T, target.T, w_query, w_key, w_value, w_out.T)])
    return grad[None], loss[0, 0]


def solution(mesh):
    in_specs = (
        P("ens", "grid", None),
        P("ens", "grid", None),
        P("grid", None),
        P("grid", None),
        P(),
        P(),
        P(),
        P(),
    )
    out_specs = (P("ens", "grid", None), P())
    return jax.shard_map(
        functools.partial(local, mesh.shape["ens"], mesh.shape["grid"]),
        mesh=mesh, in_specs=in_specs, out_specs=out_specs, check_vma=False,
    )
```

time: 45.9 us -> 35.2 us (0.77)
  local copies, waits for them, and re-layouts: 8.23 us -> 0.66 us
  Pallas kernels: 35 us -> 32.1 us
    unnamed x15 -> x1, local copies, waits for them, and re-layouts: 8.23 us -> 0.66 us
    pallas_call x1, Pallas kernels: 35 us -> 32.1 us  [local(): pl.pallas_call(functools.partial(kernel, members, regions, deep, points *...]
where the time goes in v2:
time: 35.2 us; the launch traced here: 35.1 us
  Pallas kernels  32.1 us (91%)
  between operations  2.33 us (7%)
  local copies, waits for them, and re-layouts  0.66 us (2%)
    pallas_call x1, Pallas kernels, local(): pl.pallas_call(functools.partial(kernel, members, regions, deep, points *...  32.1 us

profile of v2, /device:TPU:1, one launch (start us, length us, event | category | flops | bytes accessed | tf_op | source)
XLA Modules:
  0.0 35.1 jit_solution(7778850685887668103)
XLA Ops:
  0.6 32.1 %shard_map.95 = (f32[32,1024]{1,0:T(8,128)S(1)}, f32[1,1]{1,0:T(1,128)}) custom-call(bf16[32,1024]{1,0:T(8,128)(2,1)} %bitcast.11, bf16[256,1024]{1,0:T(8,128)(2,1)} %bitcast.8, s32[3,256]{1,0:T(4,128)} %bitcast.12, f32[100,256]{1,0:T(8,128)} %bitcast.10, bf16[1024,1024]{1,0:T(8,128)(2,1)} %wq_in.1, bf16[1024,1024]{1,0:T(8,128)(2,1)} %wk_in.1, ...), custom_call_target="tpu_custom_call" | custom-call | tf_op jit(solution)/shard_map/pallas_call | solution.py:321
  32.8 0.7 %copy.12 = f32[1,32,1024]{2,1,0:T(8,128)} copy(f32[1,32,1024]{2,1,0:T(8,128)S(1)} %bitcast.7) | data formatting | bytes 262144

commit v3 on v2

--- a/solution.py
+++ b/solution.py
@@ -32,7 +32,7 @@
     lat, feats, edges, target, wq, wk, wv, wo,
     kv, rim_out, rim_in, tpad, wof, won, query, kbd, vbd, attn, attn16, pred, got, back_out, back,
     gl, halo, plane_loss, deep_loss, mine,
-    hello, load_sem, rim_send, rim_recv, go_send, go_recv, ret_send, ret_recv,
+    hello_two, hello_four, load_sem, rim_send, rim_recv, go_send, go_recv, ret_send, ret_recv,
     halo_send, halo_recv, pl_send, pl_recv, dl_send, dl_recv,
 ):
     me = lax.axis_index("ens")
@@ -50,11 +50,15 @@
     lower = lax.rem(region + regions - 1, regions)
     upper = lax.rem(region + 1, regions)
     peers = [lax.rem(me + k, members) for k in range(members)]
+    order = sorted(range(1, members), key=lambda k: -min(k // CORES, tall - k // CORES))
     plane, line = [], []
-    for i in range(1, wide * tall):
+    def far(i, inner, outer):
+        return -min(i // inner, outer - i // inner) - (min(i % inner, inner - i % inner) if inner > CORES else 0)
+
+    for i in sorted(range(1, wide * tall), key=lambda i: far(i, tall, wide)):
         x, y = lax.rem(rx + i // tall, wide), lax.rem(ry + i % tall, tall)
         plane.append((i // tall, y * CORES + rc, x * deep + rz))
-    for i in range(1, deep * CORES):
+    for i in sorted(range(1, deep * CORES), key=lambda i: far(i, CORES, deep)):
         z, c = lax.rem(rz + i // CORES, deep), lax.rem(rc + i % CORES, CORES)
         line.append((i // CORES, ry * CORES + c, rx * deep + z))
 
@@ -69,14 +73,26 @@
             for g in range(groups)
         ]
 
+    has_lower, has_upper = region > 0, region < regions - 1
+    other = ry * CORES + lax.rem(rc + 1, CORES)
     barrier = pltpu.get_barrier_semaphore()
-    near = [
-        (ry * CORES + c, rx * deep + lax.rem(rz + step, deep)) for step in (1, deep - 1, 2, deep - 2) for c in range(CORES)
-    ]
-    greet = [(me, lower), (me, upper)] + near + [(peers[k], region) for k in range(1, members)]
-    greet += [(me, lax.rem(rx + k, wide) * deep + rz) for k in range(1, wide)]
-    for device in greet:
-        pl.semaphore_signal(barrier, inc=1, device_id=device, device_id_type=MESH)
+
+    def signal(semaphore, member, r):
+        pl.semaphore_signal(semaphore, inc=1, device_id=(member, r), device_id_type=MESH)
+
+    def at_sides(below, above):
+        pl.when(has_lower)(below)
+        pl.when(has_upper)(above)
+
+    def greet_side(r):
+        signal(barrier, me, r)
+        signal(barrier, other, r)
+
+    at_sides(lambda: greet_side(lower), lambda: greet_side(upper))
+    for k in order:
+        signal(barrier, peers[k], region)
+    for k in range(1, wide):
+        signal(barrier, me, lax.rem(rx + k, wide) * deep + rz)
 
     load_lat = load(latent_in, lat, 0)
     load_wk = load_columns(wk_in, wk, 1)
@@ -87,13 +103,34 @@
     load_wo = load(wo_in, wo, 15)
     load_target = load(target_in, target, 16)
 
-    def send(src, dst, send_sem, recv_sem, member, r):
-        copy = pltpu.make_async_remote_copy(
+    def remote(src, dst, send_sem, recv_sem, member, r):
+        return pltpu.make_async_remote_copy(
             src_ref=src, dst_ref=dst, send_sem=send_sem, recv_sem=recv_sem,
             device_id=(member, r), device_id_type=MESH,
         )
+
+    def send(*what):
+        copy = remote(*what)
         copy.start()
         return copy
+
+    def swap(low_src, low_dst, up_src, up_dst, sems):
+        down = remote(low_src, low_dst, sems[0].at[0], sems[1].at[0], me, lower)
+        up = remote(up_src, up_dst, sems[0].at[1], sems[1].at[1], me, upper)
+        at_sides(down.start, up.start)
+
+        def below():
+            down.wait_send()
+            up.wait_recv()
+
+        def above():
+            up.wait_send()
+            down.wait_recv()
+
+        def finish():
+            at_sides(below, above)
+
+        return finish
 
     load_lat.wait()
     for g in range(groups):
@@ -105,13 +142,19 @@
         rim_out[side] = jnp.concatenate(
             [kv[0, pl.ds(row, HALO), :], kv[1, pl.ds(row, HALO), :]], axis=0
         ).astype(BF16)
-    pl.semaphore_wait(barrier, len(greet))
-    rims = [
-        send(rim_out.at[0], rim_in.at[1], rim_send.at[0], rim_recv.at[0], me, lower),
-        send(rim_out.at[1], rim_in.at[0], rim_send.at[1], rim_recv.at[1], me, upper),
-    ]
-    for device in near[len(near) // 2 :]:
-        pl.semaphore_signal(hello, inc=1, device_id=device, device_id_type=MESH)
+    @pl.when(jnp.logical_not(has_lower))
+    def _():
+        rim_in[0] = jnp.zeros(rim_in.shape[1:], BF16)
+        halo[0] = jnp.zeros(halo.shape[1:], F32)
+
+    @pl.when(jnp.logical_not(has_upper))
+    def _():
+        rim_in[1] = jnp.zeros(rim_in.shape[1:], BF16)
+        halo[1] = jnp.zeros(halo.shape[1:], F32)
+
+    sides = has_lower.astype(jnp.int32) + has_upper.astype(jnp.int32)
+    pl.semaphore_wait(barrier, members - 1 + wide - 1 + CORES * sides)
+    rims = swap(rim_out.at[0], rim_in.at[1], rim_out.at[1], rim_in.at[0], (rim_send, rim_recv))
 
     load_feats.wait()
     for g in range(groups):
@@ -157,8 +200,13 @@
     won[...] = wof[...].T.astype(BF16)
     pred[...] = jnp.zeros_like(pred)
 
-    for rim in rims:
-        rim.wait()
+    rims()
+    def along(semaphore, z):
+        for c in range(CORES):
+            signal(semaphore, ry * CORES + c, rx * deep + z)
+
+    pl.when(rz >= 2)(lambda: along(hello_two, rz - 2))
+    pl.when(rz < deep - 2)(lambda: along(hello_two, rz + 2))
     for i, dst in enumerate((kbd, vbd)):
         for g in range(groups):
             cols = pl.ds(g * GROUP, GROUP)
@@ -189,12 +237,14 @@
     gone = [
         send(pred.at[pl.ds(pl.multiple_of(peers[k] * ROWS, ROWS), ROWS)], got.at[k],
              go_send.at[k], go_recv.at[k], peers[k], region)
-        for k in range(1, members)
+        for k in order
     ]
     first = pl.multiple_of(me * ROWS, ROWS)
     got[0] = pred[pl.ds(first, ROWS), :]
     for copy in gone:
         copy.wait()
+    pl.semaphore_wait(hello_two, CORES * ((rz >= 2).astype(jnp.int32) + (rz < deep - 2).astype(jnp.int32)))
+    along(hello_four, lax.rem(rz + 4, deep))
 
     coeff = 1.0 - (1.0 - ALPHA) / members
     pair = coeff / (members * (members - 1))
@@ -231,6 +281,13 @@
                 back_out[(i,) + at] = (grads[i] * (1.0 / members) - slopes[i] * pair).astype(BF16)
         loss_part = loss_part + jnp.where(valid, block_loss, 0.0)
 
+    returned = []
+    for k in order:
+        owner = lax.rem(me + members - k, members)
+        returned.append(
+            send(back_out.at[k], back.at[pl.ds(first, ROWS)],
+                 ret_send.at[k], ret_recv.at[k], owner, region)
+        )
     loss_part = jnp.sum(loss_part, axis=0, keepdims=True)
     mine[0] = loss_part
     slot = rx * tall + ry
@@ -239,17 +296,10 @@
         send(mine.at[0], plane_loss.at[slot], pl_send.at[k], pl_recv.at[k], m, r)
         for k, (_, m, r) in enumerate(plane)
     ]
-    returned = []
-    for k in range(1, members):
-        owner = lax.rem(me + members - k, members)
-        returned.append(
-            send(back_out.at[k], back.at[pl.ds(first, ROWS)],
-                 ret_send.at[k], ret_recv.at[k], owner, region)
-        )
     back[pl.ds(first, ROWS), :] = back_out[0]
+
     for copy in returned:
         copy.wait()
-
     gk, gv = [], []
     for g in range(groups):
         cols = pl.ds(g * GROUP, GROUP)
@@ -263,44 +313,53 @@
         gs = jnp.concatenate(parts, axis=0).astype(BF16)
         gk.append((gather(jnp.dot(gs, query[:, cols], preferred_element_type=F32)) * scale).astype(BF16))
         gv.append(gather(lax.dot_general(attn16[g], gc, NT, preferred_element_type=F32)).astype(BF16))
-        if g == 1:
-            pl.semaphore_wait(hello, len(near) // 2)
-            for copy in plane_sent:
-                copy.wait()
-            loss_part = plane_loss[0]
-            for k in range(1, wide * tall):
-                loss_part = loss_part + plane_loss[k]
-            mine[1] = loss_part
-            slot = rz * CORES + rc
-            deep_loss[slot] = loss_part
-            line_sent = [
-                send(mine.at[1], deep_loss.at[slot], dl_send.at[k], dl_recv.at[k], m, r)
-                for k, (_, m, r) in enumerate(line)
-            ]
     gk = jnp.concatenate(gk, axis=1)
     gv = jnp.concatenate(gv, axis=1)
+
+    for copy in plane_sent:
+        copy.wait()
+    pl.semaphore_wait(hello_four, CORES)
+    loss_part = plane_loss[0]
+    for k in range(1, wide * tall):
+        loss_part = loss_part + plane_loss[k]
+    loss_part = jnp.broadcast_to(jnp.sum(loss_part, axis=1, keepdims=True) * (1.0 / npts), loss_part.shape)
+    mine[1] = loss_part
+    slot = rz * CORES + rc
+    deep_loss[slot] = loss_part
+    line_sent = [
+        send(mine.at[1], deep_loss.at[slot], dl_send.at[k], dl_recv.at[k], m, r)
+        for k, (_, m, r) in enumerate(line)
+    ]
 
     for c in range(width // GROUP):
         cols = pl.ds(c * GROUP, GROUP)
         out = lax.dot_general(gk, wk[cols, :], NT, preferred_element_type=F32)
-        gl[:, cols] = out + lax.dot_general(gv, wv[cols, :], NT, preferred_element_type=F32)
-    rims = [
-        send(gl.at[pl.ds(own_nodes, HALO)], halo.at[1], halo_send.at[0], halo_recv.at[0], me, lower),
-        send(gl.at[pl.ds(own_nodes + HALO, HALO)], halo.at[0], halo_send.at[1], halo_recv.at[1], me, upper),
-    ]
-    grad_out[pl.ds(HALO, own_nodes - 2 * HALO), :] = gl[pl.ds(HALO, own_nodes - 2 * HALO), :]
-
-    for rim in rims:
-        rim.wait()
-    grad_out[pl.ds(0, HALO), :] = gl[pl.ds(0, HALO), :] + halo[0]
-    grad_out[pl.ds(own_nodes - HALO, HALO), :] = gl[pl.ds(own_nodes - HALO, HALO), :] + halo[1]
+        out = out + lax.dot_general(gv, wv[cols, :], NT, preferred_element_type=F32)
+        gl[:, cols] = out[own_nodes:]
+        grad_out[:, cols] = out[:own_nodes]
+    rims = swap(
+        gl.at[pl.ds(0, HALO)], halo.at[1], gl.at[pl.ds(HALO, HALO)], halo.at[0],
+        (halo_send, halo_recv),
+    )
+    rims()
+    grad_out[pl.ds(0, HALO), :] += halo[0]
+    grad_out[pl.ds(own_nodes - HALO, HALO), :] += halo[1]
 
     for copy in line_sent:
         copy.wait()
     loss_part = deep_loss[0]
     for k in range(1, deep * CORES):
         loss_part = loss_part + deep_loss[k]
-    loss_out[...] = jnp.sum(loss_part, keepdims=True) * (1.0 / npts)
+    loss_out[...] = jnp.broadcast_to(loss_part, loss_out.shape)
+
+
+def finish(grad, loss, grad_out, loss_out, one, sem):
+    copies = [pltpu.make_async_copy(grad, grad_out, sem.at[0]), pltpu.make_async_copy(one, loss_out, sem.at[1])]
+    copies[0].start()
+    one[...] = loss[pl.ds(0, 1), pl.ds(0, 1)]
+    copies[1].start()
+    for copy in copies:
+        copy.wait()
 
 
 def local(members, regions, mesh_latent, grid_feat, edges, target, w_query, w_key, w_value, w_out):
@@ -322,7 +381,7 @@
         functools.partial(kernel, members, regions, deep, points * regions * variables),
         out_shape=(
             jax.ShapeDtypeStruct((own_nodes, width), F32),
-            jax.ShapeDtypeStruct((1, 1), F32),
+            jax.ShapeDtypeStruct((8, 128), F32),
         ),
         in_specs=[any_space] * 8,
         out_specs=(vmem, vmem),
@@ -350,11 +409,12 @@
             pltpu.VMEM((members, ROWS, points), F32),
             pltpu.VMEM((members, ROWS, points), BF16),
             pltpu.VMEM((padded, points), BF16),
-            pltpu.VMEM((window, width), F32),
+            pltpu.VMEM((2 * HALO, width), F32),
             pltpu.VMEM((2, HALO, width), F32),
             pltpu.VMEM((wide * tall, 1, 128), F32),
             pltpu.VMEM((deep * CORES, 1, 128), F32),
             pltpu.VMEM((2, 1, 128), F32),
+            pltpu.SemaphoreType.REGULAR,
             pltpu.SemaphoreType.REGULAR,
             dma((17,)),
             dma((2,)), dma((2,)),
@@ -368,6 +428,17 @@
             collective_id=0, has_side_effects=True, vmem_limit_bytes=24 * 1024 * 1024
         ),
     )(*[pltpu.with_memory_space_constraint(x, pltpu.HBM) for x in (latent, feats, edges.T, target.T, w_query, w_key, w_value, w_out.T)])
+    grad, loss = pl.pallas_call(
+        finish,
+        out_shape=(
+            jax.ShapeDtypeStruct((own_nodes, width), F32),
+            jax.ShapeDtypeStruct((1, 1), F32),
+        ),
+        in_specs=[vmem, vmem],
+        out_specs=(pl.BlockSpec(memory_space=pltpu.HBM), pl.BlockSpec(memory_space=pltpu.HBM)),
+        scratch_shapes=[pltpu.VMEM((1, 1), F32), dma((2,))],
+        compiler_params=pltpu.CompilerParams(vmem_limit_bytes=4 * 1024 * 1024),
+    )(grad, loss)
     return grad[None], loss[0, 0]
 
 

time: 35.2 us -> 30.9 us (0.88)
  Pallas kernels: 32.1 us -> 30.2 us
  between operations: 2.33 us -> 0.64 us
  local copies, waits for them, and re-layouts: 0.66 us -> 0 us
    pallas_call x1, Pallas kernels: 32.1 us -> 29.5 us  [local(): pl.pallas_call(functools.partial(kernel, members, regions, deep, points *...]
    pallas_call x0 -> x1, Pallas kernels: none -> 0.68 us  [local(): pl.pallas_call(finish, out_shape=(jax.ShapeDtypeStruct((own_nodes, width)...]
    unnamed x1 -> x0, local copies, waits for them, and re-layouts: 0.66 us -> none
where the time goes in v3:
time: 30.9 us; the launch traced here: 30.8 us
  Pallas kernels  30.2 us (98%)
  between operations  0.64 us (2%)
    pallas_call x1, Pallas kernels, local(): pl.pallas_call(functools.partial(kernel, members, regions, deep, points *...  29.5 us
    pallas_call x1, Pallas kernels, local(): pl.pallas_call(finish, out_shape=(jax.ShapeDtypeStruct((own_nodes, width)...  0.68 us

profile of v3, /device:TPU:1, one launch (start us, length us, event | category | flops | bytes accessed | tf_op | source)
XLA Modules:
  0.0 30.8 jit_solution(17252390484736775456)
XLA Ops:
  0.6 29.5 %shard_map.95 = (f32[32,1024]{1,0:T(8,128)S(1)}, f32[8,128]{1,0:T(8,128)S(1)}) custom-call(bf16[32,1024]{1,0:T(8,128)(2,1)} %bitcast.10, bf16[256,1024]{1,0:T(8,128)(2,1)} %bitcast.7, s32[3,256]{1,0:T(4,128)} %bitcast.11, f32[100,256]{1,0:T(8,128)} %bitcast.9, bf16[1024,1024]{1,0:T(8,128)(2,1)} %wq_in.1, bf16[1024,1024]{1,0:T(8,128)(2,1)} %wk_in.1, ...), custom_call_target="tpu_custom_call" | custom-call | tf_op jit(solution)/shard_map/pallas_call | solution.py:380
  30.1 0.7 %shard_map.96 = (f32[32,1024]{1,0:T(8,128)}, f32[1,1]{1,0:T(1,128)}) custom-call(f32[32,1024]{1,0:T(8,128)S(1)} %get-tuple-element.6.grad, f32[8,128]{1,0:T(8,128)S(1)} %get-tuple-element.7.loss), custom_call_target="tpu_custom_call" | custom-call | tf_op jit(solution)/shard_map/pallas_call | solution.py:431

commit v4 on v3

--- a/solution.py
+++ b/solution.py
@@ -30,9 +30,9 @@
     latent_in, feats_in, edges_in, target_in, wq_in, wk_in, wv_in, wo_in,
     grad_out, loss_out,
     lat, feats, edges, target, wq, wk, wv, wo,
-    kv, rim_out, rim_in, tpad, wof, won, query, kbd, vbd, attn, attn16, pred, got, back_out, back,
+    kv, rim_out, rim_in, tpad, wof, won, query, scores, vt, vbd, attn, attn16, pred, got, back_out, back,
     gl, halo, plane_loss, deep_loss, mine,
-    hello_two, hello_four, load_sem, rim_send, rim_recv, go_send, go_recv, ret_send, ret_recv,
+    hello_one, hello_two, hello_four, load_sem, rim_send, rim_recv, go_send, go_recv, ret_send, ret_recv,
     halo_send, halo_recv, pl_send, pl_recv, dl_send, dl_recv,
 ):
     me = lax.axis_index("ens")
@@ -89,19 +89,18 @@
         signal(barrier, other, r)
 
     at_sides(lambda: greet_side(lower), lambda: greet_side(upper))
-    for k in order:
-        signal(barrier, peers[k], region)
-    for k in range(1, wide):
-        signal(barrier, me, lax.rem(rx + k, wide) * deep + rz)
+    steps_y = [lax.rem(ry + step, tall) for step in (1, tall - 1)]
+    next_x = [lax.rem(rx + step, wide) * deep + rz for step in (1, wide - 1)]
+    for y in steps_y:
+        for c in range(CORES):
+            signal(barrier, y * CORES + c, region)
+    for r in next_x:
+        signal(barrier, me, r)
+    signal(barrier, other, region)
 
     load_lat = load(latent_in, lat, 0)
     load_wk = load_columns(wk_in, wk, 1)
     load_wv = load_columns(wv_in, wv, 5)
-    load_feats = load(feats_in, feats, 9)
-    load_wq = load_columns(wq_in, wq, 10)
-    load_edges = load(edges_in, edges, 14)
-    load_wo = load(wo_in, wo, 15)
-    load_target = load(target_in, target, 16)
 
     def remote(src, dst, send_sem, recv_sem, member, r):
         return pltpu.make_async_remote_copy(
@@ -114,9 +113,12 @@
         copy.start()
         return copy
 
-    def swap(low_src, low_dst, up_src, up_dst, sems):
-        down = remote(low_src, low_dst, sems[0].at[0], sems[1].at[0], me, lower)
-        up = remote(up_src, up_dst, sems[0].at[1], sems[1].at[1], me, upper)
+    def drain(bytes_of, semaphore):
+        pltpu.make_async_copy(bytes_of, bytes_of, semaphore).wait()
+
+    def swap(low_src, low_dst, up_src, up_dst, sems, k=0):
+        down = remote(low_src, low_dst, sems[0].at[k], sems[1].at[k], me, lower)
+        up = remote(up_src, up_dst, sems[0].at[k + 1], sems[1].at[k + 1], me, upper)
         at_sides(down.start, up.start)
 
         def below():
@@ -137,6 +139,12 @@
         cols = pl.ds(g * GROUP, GROUP)
         for i, (loads, w) in enumerate(((load_wk, wk), (load_wv, wv))):
             loads[g].wait()
+            if g == groups - 1 and i == 0:
+                load_feats = load(feats_in, feats, 9)
+                load_wq = load_columns(wq_in, wq, 10)
+                load_edges = load(edges_in, edges, 14)
+                load_wo = load(wo_in, wo, 15)
+                load_target = load(target_in, target, 16)
             kv[i, :, cols] = jnp.dot(lat[...], w[:, cols], preferred_element_type=F32)
     for side, row in enumerate((0, own_nodes - HALO)):
         rim_out[side] = jnp.concatenate(
@@ -153,8 +161,13 @@
         halo[1] = jnp.zeros(halo.shape[1:], F32)
 
     sides = has_lower.astype(jnp.int32) + has_upper.astype(jnp.int32)
-    pl.semaphore_wait(barrier, members - 1 + wide - 1 + CORES * sides)
+    pl.semaphore_wait(barrier, 2 * CORES + 2 + 1 + CORES * sides)
     rims = swap(rim_out.at[0], rim_in.at[1], rim_out.at[1], rim_in.at[0], (rim_send, rim_recv))
+
+    for y in steps_y:
+        signal(hello_one, y * CORES + rc, region)
+    for r in next_x:
+        signal(hello_one, me, r)
 
     load_feats.wait()
     for g in range(groups):
@@ -181,15 +194,30 @@
         return jnp.where(head_of(x.shape[0]) == h, x, 0.0).astype(BF16)
 
     def gather(x):
-        out = jnp.zeros((window, GROUP), F32)
+        own, rim = x[:own_nodes], x[heads * own_nodes : heads * own_nodes + 2 * HALO]
+        for h in range(1, heads):
+            at = heads * own_nodes + h * 2 * HALO
+            own = jnp.where(head_of(own_nodes) == h, x[h * own_nodes : (h + 1) * own_nodes], own)
+            rim = jnp.where(head_of(2 * HALO) == h, x[at : at + 2 * HALO], rim)
+        return jnp.concatenate([own, rim], axis=0)
+
+    def fold(op, reduce, own, rim):
+        pieces = [x[i : i + 8] for x in (own, rim) for i in range(0, x.shape[0], 8)]
+        while len(pieces) > 1:
+            pieces = [op(*pair) for pair in zip(pieces[::2], pieces[1::2])] + pieces[len(pieces) // 2 * 2 :]
+        return reduce(pieces[0], axis=0, keepdims=True)
+
+    stacked = heads * own_nodes
+    for g in range(groups):
+        cols = pl.ds(g * GROUP, GROUP)
+        kb = jnp.concatenate([spread(kv[0, :, cols], h) for h in range(heads)], axis=0)
+        vb = jnp.concatenate([spread(kv[1, :, cols], h) for h in range(heads)], axis=0)
+        vbd[g, pl.ds(0, stacked), :] = vb
+        vt[g, :, pl.ds(0, stacked)] = vb.T
+        own = lax.dot_general(kb, query[:, cols], NT, preferred_element_type=F32)
         for h in range(heads):
-            out = jnp.where(head_of(window) == h, x[h * window : (h + 1) * window], out)
-        return out
-
-    for g in range(groups):
-        for h in range(heads):
-            for i, dst in enumerate((kbd, vbd)):
-                dst[g, pl.ds(h * window, own_nodes), :] = spread(kv[i, :, pl.ds(g * GROUP, GROUP)], h)
+            rows = slice(h * own_nodes, (h + 1) * own_nodes)
+            scores[g, rows, :] = jnp.where(linked[:own_nodes], own[rows], -jnp.inf)
 
     load_target.wait()
     load_wo.wait()
@@ -207,42 +235,52 @@
 
     pl.when(rz >= 2)(lambda: along(hello_two, rz - 2))
     pl.when(rz < deep - 2)(lambda: along(hello_two, rz + 2))
-    for i, dst in enumerate((kbd, vbd)):
-        for g in range(groups):
-            cols = pl.ds(g * GROUP, GROUP)
-            both = jnp.concatenate(
+    rim_scores = []
+    for g in range(groups):
+        cols = pl.ds(g * GROUP, GROUP)
+        both = [
+            jnp.concatenate(
                 [rim_in[side, :, cols].astype(F32)[i * HALO : (i + 1) * HALO] for side in range(2)], axis=0
             )
-            for h in range(heads):
-                dst[g, pl.ds(h * window + own_nodes, 2 * HALO), :] = spread(both, h)
+            for i in range(2)
+        ]
+        kb = jnp.concatenate([spread(both[0], h) for h in range(heads)], axis=0)
+        vb = jnp.concatenate([spread(both[1], h) for h in range(heads)], axis=0)
+        rim_scores.append(lax.dot_general(kb, query[:, cols], NT, preferred_element_type=F32))
+        vbd[g, pl.ds(stacked, heads * 2 * HALO), :] = vb
+        vt[g, :, pl.ds(stacked, heads * 2 * HALO)] = vb.T
     total = jnp.zeros((variables, points), F32)
     scale = head_size ** (-0.5)
     for g in range(groups):
         cols = pl.ds(g * GROUP, GROUP)
-        scores = lax.dot_general(kbd[g], query[:, cols], NT, preferred_element_type=F32)
-        parts = []
+        parts, rim_parts = [], []
         for h in range(heads):
-            s = jnp.where(linked, scores[h * window : (h + 1) * window], -jnp.inf)
-            top = jnp.max(s, axis=0, keepdims=True)
-            e = count * jnp.exp2((s - top) * (scale * LOG2E))
-            a = e * (1.0 / jnp.sum(e, axis=0, keepdims=True))
-            attn[g, pl.ds(h * window, window), :] = a
-            parts.append(a.astype(BF16))
-        a16 = jnp.concatenate(parts, axis=0)
+            rows = pl.ds(h * own_nodes, own_nodes)
+            s = scores[g, rows, :]
+            r = jnp.where(linked[own_nodes:], rim_scores[g][h * 2 * HALO : (h + 1) * 2 * HALO], -jnp.inf)
+            top = fold(jnp.maximum, jnp.max, s, r)
+            e = count[:own_nodes] * jnp.exp2((s - top) * (scale * LOG2E))
+            f = count[own_nodes:] * jnp.exp2((r - top) * (scale * LOG2E))
+            inv = 1.0 / fold(jnp.add, jnp.sum, e, f)
+            e, f = e * inv, f * inv
+            attn[g, rows, :] = e
+            attn[g, pl.ds(stacked + h * 2 * HALO, 2 * HALO), :] = f
+            parts.append(e.astype(BF16))
+            rim_parts.append(f.astype(BF16))
+        a16 = jnp.concatenate(parts + rim_parts, axis=0)
         attn16[g] = a16
-        ctx = lax.dot_general(vbd[g], a16, TN, preferred_element_type=F32).astype(BF16)
+        ctx = jnp.dot(vt[g], a16, preferred_element_type=F32).astype(BF16)
         total = total + jnp.dot(wo[:, cols], ctx, preferred_element_type=F32)
     pred[pl.ds(0, variables), :] = total
 
-    gone = [
+    pl.semaphore_wait(hello_one, 4)
+    for k in order:
         send(pred.at[pl.ds(pl.multiple_of(peers[k] * ROWS, ROWS), ROWS)], got.at[k],
-             go_send.at[k], go_recv.at[k], peers[k], region)
-        for k in order
-    ]
+             go_send, go_recv, peers[k], region)
     first = pl.multiple_of(me * ROWS, ROWS)
     got[0] = pred[pl.ds(first, ROWS), :]
-    for copy in gone:
-        copy.wait()
+    drain(got.at[pl.ds(1, members - 1)], go_send)
+    drain(got.at[pl.ds(1, members - 1)], go_recv)
     pl.semaphore_wait(hello_two, CORES * ((rz >= 2).astype(jnp.int32) + (rz < deep - 2).astype(jnp.int32)))
     along(hello_four, lax.rem(rz + 4, deep))
 
@@ -281,43 +319,45 @@
                 back_out[(i,) + at] = (grads[i] * (1.0 / members) - slopes[i] * pair).astype(BF16)
         loss_part = loss_part + jnp.where(valid, block_loss, 0.0)
 
-    returned = []
     for k in order:
         owner = lax.rem(me + members - k, members)
-        returned.append(
-            send(back_out.at[k], back.at[pl.ds(first, ROWS)],
-                 ret_send.at[k], ret_recv.at[k], owner, region)
-        )
+        send(back_out.at[k], back.at[pl.ds(first, ROWS)], ret_send, ret_recv, owner, region)
     loss_part = jnp.sum(loss_part, axis=0, keepdims=True)
     mine[0] = loss_part
     slot = rx * tall + ry
     plane_loss[slot] = loss_part
-    plane_sent = [
-        send(mine.at[0], plane_loss.at[slot], pl_send.at[k], pl_recv.at[k], m, r)
-        for k, (_, m, r) in enumerate(plane)
-    ]
+    for _, m, r in plane:
+        send(mine.at[0], plane_loss.at[slot], pl_send, pl_recv, m, r)
     back[pl.ds(first, ROWS), :] = back_out[0]
 
-    for copy in returned:
-        copy.wait()
-    gk, gv = [], []
+    drain(back_out.at[pl.ds(1, members - 1)], ret_send)
+    drain(back_out.at[pl.ds(1, members - 1)], ret_recv)
+    gcs, gas, gk, gv = [], [], [], []
+    for g in range(groups):
+        gc = jnp.dot(won[pl.ds(g * GROUP, GROUP), :], back[...], preferred_element_type=F32).astype(BF16)
+        gcs.append(gc)
+    for g in range(groups):
+        gas.append(jnp.dot(vbd[g], gcs[g], preferred_element_type=F32))
+    for g in range(groups):
+        gv.append(gather(lax.dot_general(attn16[g], gcs[g], NT, preferred_element_type=F32)).astype(BF16))
     for g in range(groups):
         cols = pl.ds(g * GROUP, GROUP)
-        gc = jnp.dot(won[cols, :], back[...], preferred_element_type=F32).astype(BF16)
-        ga = jnp.dot(vbd[g], gc, preferred_element_type=F32)
-        parts = []
+        ga = gas[g]
+        parts, rim_parts = [], []
         for h in range(heads):
-            a = attn[g, pl.ds(h * window, window), :]
-            t = a * ga[h * window : (h + 1) * window]
-            parts.append(t - a * jnp.sum(t, axis=0, keepdims=True))
-        gs = jnp.concatenate(parts, axis=0).astype(BF16)
+            at = stacked + h * 2 * HALO
+            a, f = attn[g, pl.ds(h * own_nodes, own_nodes), :], attn[g, pl.ds(at, 2 * HALO), :]
+            t, u = a * ga[h * own_nodes : (h + 1) * own_nodes], f * ga[at : at + 2 * HALO]
+            mean = fold(jnp.add, jnp.sum, t, u)
+            parts.append(t - a * mean)
+            rim_parts.append(u - f * mean)
+        gs = jnp.concatenate(parts + rim_parts, axis=0).astype(BF16)
         gk.append((gather(jnp.dot(gs, query[:, cols], preferred_element_type=F32)) * scale).astype(BF16))
-        gv.append(gather(lax.dot_general(attn16[g], gc, NT, preferred_element_type=F32)).astype(BF16))
     gk = jnp.concatenate(gk, axis=1)
     gv = jnp.concatenate(gv, axis=1)
 
-    for copy in plane_sent:
-        copy.wait()
+    drain(plane_loss.at[pl.ds(1, len(plane))], pl_send)
+    drain(plane_loss.at[pl.ds(1, len(plane))], pl_recv)
     pl.semaphore_wait(hello_four, CORES)
     loss_part = plane_loss[0]
     for k in range(1, wide * tall):
@@ -326,27 +366,29 @@
     mine[1] = loss_part
     slot = rz * CORES + rc
     deep_loss[slot] = loss_part
-    line_sent = [
-        send(mine.at[1], deep_loss.at[slot], dl_send.at[k], dl_recv.at[k], m, r)
-        for k, (_, m, r) in enumerate(line)
-    ]
-
+    for _, m, r in line:
+        send(mine.at[1], deep_loss.at[slot], dl_send, dl_recv, m, r)
+
+    rims = []
     for c in range(width // GROUP):
         cols = pl.ds(c * GROUP, GROUP)
         out = lax.dot_general(gk, wk[cols, :], NT, preferred_element_type=F32)
         out = out + lax.dot_general(gv, wv[cols, :], NT, preferred_element_type=F32)
         gl[:, cols] = out[own_nodes:]
         grad_out[:, cols] = out[:own_nodes]
-    rims = swap(
-        gl.at[pl.ds(0, HALO)], halo.at[1], gl.at[pl.ds(HALO, HALO)], halo.at[0],
-        (halo_send, halo_recv),
-    )
-    rims()
+        if c % 2:
+            half = pl.ds((c - 1) * GROUP, 2 * GROUP)
+            rims.append(swap(
+                gl.at[pl.ds(0, HALO), half], halo.at[1, :, half],
+                gl.at[pl.ds(HALO, HALO), half], halo.at[0, :, half], (halo_send, halo_recv), c - 1,
+            ))
+    for finish_rims in rims:
+        finish_rims()
     grad_out[pl.ds(0, HALO), :] += halo[0]
     grad_out[pl.ds(own_nodes - HALO, HALO), :] += halo[1]
 
-    for copy in line_sent:
-        copy.wait()
+    drain(deep_loss.at[pl.ds(1, len(line))], dl_send)
+    drain(deep_loss.at[pl.ds(1, len(line))], dl_recv)
     loss_part = deep_loss[0]
     for k in range(1, deep * CORES):
         loss_part = loss_part + deep_loss[k]
@@ -401,7 +443,8 @@
             pltpu.VMEM((padded, width), F32),
             pltpu.VMEM((width, padded), BF16),
             pltpu.VMEM((points, width), BF16),
-            pltpu.VMEM((groups, stack, GROUP), BF16),
+            pltpu.VMEM((groups, stack, points), F32),
+            pltpu.VMEM((groups, GROUP, stack), BF16),
             pltpu.VMEM((groups, stack, GROUP), BF16),
             pltpu.VMEM((groups, stack, points), F32),
             pltpu.VMEM((groups, stack, points), BF16),
@@ -416,13 +459,14 @@
             pltpu.VMEM((2, 1, 128), F32),
             pltpu.SemaphoreType.REGULAR,
             pltpu.SemaphoreType.REGULAR,
+            pltpu.SemaphoreType.REGULAR,
             dma((17,)),
             dma((2,)), dma((2,)),
-            dma((members,)), dma((members,)),
-            dma((members,)), dma((members,)),
-            dma((2,)), dma((2,)),
-            dma((wide * tall,)), dma((wide * tall,)),
-            dma((deep * CORES,)), dma((deep * CORES,)),
+            dma, dma,
+            dma, dma,
+            dma((4,)), dma((4,)),
+            dma, dma,
+            dma, dma,
         ],
         compiler_params=pltpu.CompilerParams(
             collective_id=0, has_side_effects=True, vmem_limit_bytes=24 * 1024 * 1024

time: 30.9 us -> 29.8 us (0.964)
  Pallas kernels: 30.2 us -> 29.1 us
    pallas_call x1, Pallas kernels: 29.5 us -> 28.4 us  [local(): pl.pallas_call(functools.partial(kernel, members, regions, deep, points *...]
where the time goes in v4:
time: 29.8 us; the launch traced here: 29.7 us
  Pallas kernels  29.1 us (98%)
  between operations  0.64 us (2%)
    pallas_call x1, Pallas kernels, local(): pl.pallas_call(functools.partial(kernel, members, regions, deep, points *...  28.4 us
    pallas_call x1, Pallas kernels, local(): pl.pallas_call(finish, out_shape=(jax.ShapeDtypeStruct((own_nodes, width)...  0.68 us

profile of v4, /device:TPU:1, one launch (start us, length us, event | category | flops | bytes accessed | tf_op | source)
XLA Modules:
  0.0 29.7 jit_solution(17797551547150989281)
XLA Ops:
  0.6 28.4 %shard_map.95 = (f32[32,1024]{1,0:T(8,128)S(1)}, f32[8,128]{1,0:T(8,128)S(1)}) custom-call(bf16[32,1024]{1,0:T(8,128)(2,1)} %bitcast.10, bf16[256,1024]{1,0:T(8,128)(2,1)} %bitcast.7, s32[3,256]{1,0:T(4,128)} %bitcast.11, f32[100,256]{1,0:T(8,128)} %bitcast.9, bf16[1024,1024]{1,0:T(8,128)(2,1)} %wq_in.1, bf16[1024,1024]{1,0:T(8,128)(2,1)} %wk_in.1, ...), custom_call_target="tpu_custom_call" | custom-call | tf_op jit(solution)/shard_map/pallas_call | solution.py:422
  29.1 0.7 %shard_map.96 = (f32[32,1024]{1,0:T(8,128)}, f32[1,1]{1,0:T(1,128)}) custom-call(f32[32,1024]{1,0:T(8,128)S(1)} %get-tuple-element.6.grad, f32[8,128]{1,0:T(8,128)S(1)} %get-tuple-element.7.loss), custom_call_target="tpu_custom_call" | custom-call | tf_op jit(solution)/shard_map/pallas_call | solution.py:475

commit v5 on v4

--- a/solution.py
+++ b/solution.py
@@ -68,9 +68,9 @@
         return copy
 
     def load_columns(src, dst, k):
+        half = width // 2
         return [
-            load(src.at[:, pl.ds(g * GROUP, GROUP)], dst.at[:, pl.ds(g * GROUP, GROUP)], k + g)
-            for g in range(groups)
+            load(src.at[:, pl.ds(i * half, half)], dst.at[:, pl.ds(i * half, half)], k + i) for i in range(2)
         ]
 
     has_lower, has_upper = region > 0, region < regions - 1
@@ -100,7 +100,7 @@
 
     load_lat = load(latent_in, lat, 0)
     load_wk = load_columns(wk_in, wk, 1)
-    load_wv = load_columns(wv_in, wv, 5)
+    load_wv = load_columns(wv_in, wv, 3)
 
     def remote(src, dst, send_sem, recv_sem, member, r):
         return pltpu.make_async_remote_copy(
@@ -138,13 +138,14 @@
     for g in range(groups):
         cols = pl.ds(g * GROUP, GROUP)
         for i, (loads, w) in enumerate(((load_wk, wk), (load_wv, wv))):
-            loads[g].wait()
-            if g == groups - 1 and i == 0:
-                load_feats = load(feats_in, feats, 9)
-                load_wq = load_columns(wq_in, wq, 10)
-                load_edges = load(edges_in, edges, 14)
-                load_wo = load(wo_in, wo, 15)
-                load_target = load(target_in, target, 16)
+            if g % 2 == 0:
+                loads[g // 2].wait()
+            if g == groups - 2 and i == 0:
+                load_feats = load(feats_in, feats, 5)
+                load_wq = load_columns(wq_in, wq, 6)
+                load_edges = load(edges_in, edges, 8)
+                load_wo = load(wo_in, wo, 9)
+                load_target = load(target_in, target, 10)
             kv[i, :, cols] = jnp.dot(lat[...], w[:, cols], preferred_element_type=F32)
     for side, row in enumerate((0, own_nodes - HALO)):
         rim_out[side] = jnp.concatenate(
@@ -172,7 +173,8 @@
     load_feats.wait()
     for g in range(groups):
         cols = pl.ds(g * GROUP, GROUP)
-        load_wq[g].wait()
+        if g % 2 == 0:
+            load_wq[g // 2].wait()
         query[:, cols] = jnp.dot(
             feats[...], wq[:, cols], preferred_element_type=F32
         ).astype(BF16)
@@ -249,10 +251,9 @@
         rim_scores.append(lax.dot_general(kb, query[:, cols], NT, preferred_element_type=F32))
         vbd[g, pl.ds(stacked, heads * 2 * HALO), :] = vb
         vt[g, :, pl.ds(stacked, heads * 2 * HALO)] = vb.T
-    total = jnp.zeros((variables, points), F32)
     scale = head_size ** (-0.5)
-    for g in range(groups):
-        cols = pl.ds(g * GROUP, GROUP)
+
+    def attend(g):
         parts, rim_parts = [], []
         for h in range(heads):
             rows = pl.ds(h * own_nodes, own_nodes)
@@ -269,8 +270,18 @@
             rim_parts.append(f.astype(BF16))
         a16 = jnp.concatenate(parts + rim_parts, axis=0)
         attn16[g] = a16
-        ctx = jnp.dot(vt[g], a16, preferred_element_type=F32).astype(BF16)
-        total = total + jnp.dot(wo[:, cols], ctx, preferred_element_type=F32)
+        return a16
+
+    total = jnp.zeros((variables, points), F32)
+    weights, contexts = {}, {}
+    for step in range(groups + 2):
+        if step < groups:
+            weights[step] = attend(step)
+        if 0 <= step - 1 < groups:
+            contexts[step - 1] = jnp.dot(vt[step - 1], weights[step - 1], preferred_element_type=F32).astype(BF16)
+        if 0 <= step - 2:
+            g = step - 2
+            total = total + jnp.dot(wo[:, pl.ds(g * GROUP, GROUP)], contexts[g], preferred_element_type=F32)
     pred[pl.ds(0, variables), :] = total
 
     pl.semaphore_wait(hello_one, 4)
@@ -319,16 +330,29 @@
                 back_out[(i,) + at] = (grads[i] * (1.0 / members) - slopes[i] * pair).astype(BF16)
         loss_part = loss_part + jnp.where(valid, block_loss, 0.0)
 
-    for k in order:
-        owner = lax.rem(me + members - k, members)
-        send(back_out.at[k], back.at[pl.ds(first, ROWS)], ret_send, ret_recv, owner, region)
     loss_part = jnp.sum(loss_part, axis=0, keepdims=True)
     mine[0] = loss_part
     slot = rx * tall + ry
     plane_loss[slot] = loss_part
     for _, m, r in plane:
         send(mine.at[0], plane_loss.at[slot], pl_send, pl_recv, m, r)
+    for k in order:
+        owner = lax.rem(me + members - k, members)
+        send(back_out.at[k], back.at[pl.ds(first, ROWS)], ret_send, ret_recv, owner, region)
     back[pl.ds(first, ROWS), :] = back_out[0]
+
+    drain(plane_loss.at[pl.ds(1, len(plane))], pl_send)
+    drain(plane_loss.at[pl.ds(1, len(plane))], pl_recv)
+    pl.semaphore_wait(hello_four, CORES)
+    loss_part = plane_loss[0]
+    for k in range(1, wide * tall):
+        loss_part = loss_part + plane_loss[k]
+    loss_part = jnp.broadcast_to(jnp.sum(loss_part, axis=1, keepdims=True) * (1.0 / npts), loss_part.shape)
+    mine[1] = loss_part
+    slot = rz * CORES + rc
+    deep_loss[slot] = loss_part
+    for _, m, r in line:
+        send(mine.at[1], deep_loss.at[slot], dl_send, dl_recv, m, r)
 
     drain(back_out.at[pl.ds(1, members - 1)], ret_send)
     drain(back_out.at[pl.ds(1, members - 1)], ret_recv)
@@ -356,34 +380,16 @@
     gk = jnp.concatenate(gk, axis=1)
     gv = jnp.concatenate(gv, axis=1)
 
-    drain(plane_loss.at[pl.ds(1, len(plane))], pl_send)
-    drain(plane_loss.at[pl.ds(1, len(plane))], pl_recv)
-    pl.semaphore_wait(hello_four, CORES)
-    loss_part = plane_loss[0]
-    for k in range(1, wide * tall):
-        loss_part = loss_part + plane_loss[k]
-    loss_part = jnp.broadcast_to(jnp.sum(loss_part, axis=1, keepdims=True) * (1.0 / npts), loss_part.shape)
-    mine[1] = loss_part
-    slot = rz * CORES + rc
-    deep_loss[slot] = loss_part
-    for _, m, r in line:
-        send(mine.at[1], deep_loss.at[slot], dl_send, dl_recv, m, r)
-
-    rims = []
     for c in range(width // GROUP):
         cols = pl.ds(c * GROUP, GROUP)
         out = lax.dot_general(gk, wk[cols, :], NT, preferred_element_type=F32)
         out = out + lax.dot_general(gv, wv[cols, :], NT, preferred_element_type=F32)
         gl[:, cols] = out[own_nodes:]
         grad_out[:, cols] = out[:own_nodes]
-        if c % 2:
-            half = pl.ds((c - 1) * GROUP, 2 * GROUP)
-            rims.append(swap(
-                gl.at[pl.ds(0, HALO), half], halo.at[1, :, half],
-                gl.at[pl.ds(HALO, HALO), half], halo.at[0, :, half], (halo_send, halo_recv), c - 1,
-            ))
-    for finish_rims in rims:
-        finish_rims()
+    rims = swap(
+        gl.at[pl.ds(0, HALO)], halo.at[1], gl.at[pl.ds(HALO, HALO)], halo.at[0], (halo_send, halo_recv)
+    )
+    rims()
     grad_out[pl.ds(0, HALO), :] += halo[0]
     grad_out[pl.ds(own_nodes - HALO, HALO), :] += halo[1]
 
@@ -460,11 +466,11 @@
             pltpu.SemaphoreType.REGULAR,
             pltpu.SemaphoreType.REGULAR,
             pltpu.SemaphoreType.REGULAR,
-            dma((17,)),
+            dma((11,)),
             dma((2,)), dma((2,)),
             dma, dma,
             dma, dma,
-            dma((4,)), dma((4,)),
+            dma((2,)), dma((2,)),
             dma, dma,
             dma, dma,
         ],

time: 29.8 us -> 29.3 us (0.983)
  Pallas kernels: 29.1 us -> 28.5 us
    pallas_call x1, Pallas kernels: 28.4 us -> 27.8 us  [local(): pl.pallas_call(functools.partial(kernel, members, regions, deep, points *...]
where the time goes in v5:
time: 29.3 us; the launch traced here: 29.2 us
  Pallas kernels  28.5 us (97%)
  between operations  0.64 us (2%)
    pallas_call x1, Pallas kernels, local(): pl.pallas_call(functools.partial(kernel, members, regions, deep, points *...  27.8 us
    pallas_call x1, Pallas kernels, local(): pl.pallas_call(finish, out_shape=(jax.ShapeDtypeStruct((own_nodes, width)...  0.68 us

profile of v5, /device:TPU:1, one launch (start us, length us, event | category | flops | bytes accessed | tf_op | source)
XLA Modules:
  0.0 29.2 jit_solution(12235998537710473195)
XLA Ops:
  0.6 27.8 %shard_map.95 = (f32[32,1024]{1,0:T(8,128)S(1)}, f32[8,128]{1,0:T(8,128)S(1)}) custom-call(bf16[32,1024]{1,0:T(8,128)(2,1)} %bitcast.10, bf16[256,1024]{1,0:T(8,128)(2,1)} %bitcast.7, s32[3,256]{1,0:T(4,128)} %bitcast.11, f32[100,256]{1,0:T(8,128)} %bitcast.9, bf16[1024,1024]{1,0:T(8,128)(2,1)} %wq_in.1, bf16[1024,1024]{1,0:T(8,128)(2,1)} %wk_in.1, ...), custom_call_target="tpu_custom_call" | custom-call | tf_op jit(solution)/shard_map/pallas_call | solution.py:428
  28.5 0.7 %shard_map.96 = (f32[32,1024]{1,0:T(8,128)}, f32[1,1]{1,0:T(1,128)}) custom-call(f32[32,1024]{1,0:T(8,128)S(1)} %get-tuple-element.6.grad, f32[8,128]{1,0:T(8,128)S(1)} %get-tuple-element.7.loss), custom_call_target="tpu_custom_call" | custom-call | tf_op jit(solution)/shard_map/pallas_call | solution.py:481

commit v6 on v5

--- a/solution.py
+++ b/solution.py
@@ -30,7 +30,7 @@
     latent_in, feats_in, edges_in, target_in, wq_in, wk_in, wv_in, wo_in,
     grad_out, loss_out,
     lat, feats, edges, target, wq, wk, wv, wo,
-    kv, rim_out, rim_in, tpad, wof, won, query, scores, vt, vbd, attn, attn16, pred, got, back_out, back,
+    kv, rim_out, rim_in, tpad, wof, won, query, scores, tops, sums, vt, vbd, attn, attn16, pred, got, back_out, back,
     gl, halo, plane_loss, deep_loss, mine,
     hello_one, hello_two, hello_four, load_sem, rim_send, rim_recv, go_send, go_recv, ret_send, ret_recv,
     halo_send, halo_recv, pl_send, pl_recv, dl_send, dl_recv,
@@ -203,12 +203,13 @@
             rim = jnp.where(head_of(2 * HALO) == h, x[at : at + 2 * HALO], rim)
         return jnp.concatenate([own, rim], axis=0)
 
-    def fold(op, reduce, own, rim):
-        pieces = [x[i : i + 8] for x in (own, rim) for i in range(0, x.shape[0], 8)]
+    def fold(op, reduce, *arrays):
+        pieces = [x[i : i + 8] for x in arrays for i in range(0, x.shape[0], 8)]
         while len(pieces) > 1:
             pieces = [op(*pair) for pair in zip(pieces[::2], pieces[1::2])] + pieces[len(pieces) // 2 * 2 :]
         return reduce(pieces[0], axis=0, keepdims=True)
 
+    scale = head_size ** (-0.5)
     stacked = heads * own_nodes
     for g in range(groups):
         cols = pl.ds(g * GROUP, GROUP)
@@ -219,7 +220,12 @@
         own = lax.dot_general(kb, query[:, cols], NT, preferred_element_type=F32)
         for h in range(heads):
             rows = slice(h * own_nodes, (h + 1) * own_nodes)
-            scores[g, rows, :] = jnp.where(linked[:own_nodes], own[rows], -jnp.inf)
+            s = jnp.where(linked[:own_nodes], own[rows], -jnp.inf)
+            top = jnp.maximum(fold(jnp.maximum, jnp.max, s), -1e30)
+            e = count[:own_nodes] * jnp.exp2((s - top) * (scale * LOG2E))
+            scores[g, rows, :] = e
+            tops[g * heads + h] = top
+            sums[g * heads + h] = fold(jnp.add, jnp.sum, e)
 
     load_target.wait()
     load_wo.wait()
@@ -251,19 +257,17 @@
         rim_scores.append(lax.dot_general(kb, query[:, cols], NT, preferred_element_type=F32))
         vbd[g, pl.ds(stacked, heads * 2 * HALO), :] = vb
         vt[g, :, pl.ds(stacked, heads * 2 * HALO)] = vb.T
-    scale = head_size ** (-0.5)
-
     def attend(g):
         parts, rim_parts = [], []
         for h in range(heads):
             rows = pl.ds(h * own_nodes, own_nodes)
-            s = scores[g, rows, :]
+            own_top = tops[g * heads + h]
             r = jnp.where(linked[own_nodes:], rim_scores[g][h * 2 * HALO : (h + 1) * 2 * HALO], -jnp.inf)
-            top = fold(jnp.maximum, jnp.max, s, r)
-            e = count[:own_nodes] * jnp.exp2((s - top) * (scale * LOG2E))
+            top = jnp.maximum(own_top, fold(jnp.maximum, jnp.max, r))
+            weight = jnp.exp2((own_top - top) * (scale * LOG2E))
             f = count[own_nodes:] * jnp.exp2((r - top) * (scale * LOG2E))
-            inv = 1.0 / fold(jnp.add, jnp.sum, e, f)
-            e, f = e * inv, f * inv
+            inv = 1.0 / (sums[g * heads + h] * weight + fold(jnp.add, jnp.sum, f))
+            e, f = scores[g, rows, :] * (weight * inv), f * inv
             attn[g, rows, :] = e
             attn[g, pl.ds(stacked + h * 2 * HALO, 2 * HALO), :] = f
             parts.append(e.astype(BF16))
@@ -450,6 +454,8 @@
             pltpu.VMEM((width, padded), BF16),
             pltpu.VMEM((points, width), BF16),
             pltpu.VMEM((groups, stack, points), F32),
+            pltpu.VMEM((HEADS, 1, points), F32),
+            pltpu.VMEM((HEADS, 1, points), F32),
             pltpu.VMEM((groups, GROUP, stack), BF16),
             pltpu.VMEM((groups, stack, GROUP), BF16),
             pltpu.VMEM((groups, stack, points), F32),

time: 29.3 us -> 29.3 us (level)
  no operation moved by 1% of the time
where the time goes in v6:
time: 29.3 us; the launch traced here: 29.1 us
  Pallas kernels  28.4 us (97%)
  between operations  0.64 us (2%)
    pallas_call x1, Pallas kernels, local(): pl.pallas_call(functools.partial(kernel, members, regions, deep, points *...  27.8 us
    pallas_call x1, Pallas kernels, local(): pl.pallas_call(finish, out_shape=(jax.ShapeDtypeStruct((own_nodes, width)...  0.68 us

profile of v6, /device:TPU:1, one launch (start us, length us, event | category | flops | bytes accessed | tf_op | source)
XLA Modules:
  0.0 29.1 jit_solution(251663474565721636)
XLA Ops:
  0.6 27.8 %shard_map.95 = (f32[32,1024]{1,0:T(8,128)S(1)}, f32[8,128]{1,0:T(8,128)S(1)}) custom-call(bf16[32,1024]{1,0:T(8,128)(2,1)} %bitcast.10, bf16[256,1024]{1,0:T(8,128)(2,1)} %bitcast.7, s32[3,256]{1,0:T(4,128)} %bitcast.11, f32[100,256]{1,0:T(8,128)} %bitcast.9, bf16[1024,1024]{1,0:T(8,128)(2,1)} %wq_in.1, bf16[1024,1024]{1,0:T(8,128)(2,1)} %wk_in.1, ...), custom_call_target="tpu_custom_call" | custom-call | tf_op jit(solution)/shard_map/pallas_call | solution.py:432
  28.4 0.7 %shard_map.96 = (f32[32,1024]{1,0:T(8,128)}, f32[1,1]{1,0:T(1,128)}) custom-call(f32[32,1024]{1,0:T(8,128)S(1)} %get-tuple-element.6.grad, f32[8,128]{1,0:T(8,128)S(1)} %get-tuple-element.7.loss), custom_call_target="tpu_custom_call" | custom-call | tf_op jit(solution)/shard_map/pallas_call | solution.py:487

commit v7 on v6

--- a/solution.py
+++ b/solution.py
@@ -67,12 +67,6 @@
         copy.start()
         return copy
 
-    def load_columns(src, dst, k):
-        half = width // 2
-        return [
-            load(src.at[:, pl.ds(i * half, half)], dst.at[:, pl.ds(i * half, half)], k + i) for i in range(2)
-        ]
-
     has_lower, has_upper = region > 0, region < regions - 1
     other = ry * CORES + lax.rem(rc + 1, CORES)
     barrier = pltpu.get_barrier_semaphore()
@@ -99,8 +93,8 @@
     signal(barrier, other, region)
 
     load_lat = load(latent_in, lat, 0)
-    load_wk = load_columns(wk_in, wk, 1)
-    load_wv = load_columns(wv_in, wv, 3)
+    load_wk = load(wk_in, wk, 1)
+    load_wv = load(wv_in, wv, 2)
 
     def remote(src, dst, send_sem, recv_sem, member, r):
         return pltpu.make_async_remote_copy(
@@ -135,17 +129,16 @@
         return finish
 
     load_lat.wait()
+    load_wk.wait()
+    load_feats = load(feats_in, feats, 3)
+    load_wq = load(wq_in, wq, 4)
+    load_edges = load(edges_in, edges, 5)
+    load_wo = load(wo_in, wo, 6)
+    load_target = load(target_in, target, 7)
+    load_wv.wait()
     for g in range(groups):
         cols = pl.ds(g * GROUP, GROUP)
-        for i, (loads, w) in enumerate(((load_wk, wk), (load_wv, wv))):
-            if g % 2 == 0:
-                loads[g // 2].wait()
-            if g == groups - 2 and i == 0:
-                load_feats = load(feats_in, feats, 5)
-                load_wq = load_columns(wq_in, wq, 6)
-                load_edges = load(edges_in, edges, 8)
-                load_wo = load(wo_in, wo, 9)
-                load_target = load(target_in, target, 10)
+        for i, w in enumerate((wk, wv)):
             kv[i, :, cols] = jnp.dot(lat[...], w[:, cols], preferred_element_type=F32)
     for side, row in enumerate((0, own_nodes - HALO)):
         rim_out[side] = jnp.concatenate(
@@ -171,10 +164,9 @@
         signal(hello_one, me, r)
 
     load_feats.wait()
+    load_wq.wait()
     for g in range(groups):
         cols = pl.ds(g * GROUP, GROUP)
-        if g % 2 == 0:
-            load_wq[g // 2].wait()
         query[:, cols] = jnp.dot(
             feats[...], wq[:, cols], preferred_element_type=F32
         ).astype(BF16)
@@ -472,7 +464,7 @@
             pltpu.SemaphoreType.REGULAR,
             pltpu.SemaphoreType.REGULAR,
             pltpu.SemaphoreType.REGULAR,
-            dma((11,)),
+            dma((8,)),
             dma((2,)), dma((2,)),
             dma, dma,
             dma, dma,

time: 29.3 us -> 29.3 us (level)
  no operation moved by 1% of the time
where the time goes in v7:
time: 29.3 us; the launch traced here: 29.2 us
  Pallas kernels  28.6 us (98%)
  between operations  0.64 us (2%)
    pallas_call x1, Pallas kernels, local(): pl.pallas_call(functools.partial(kernel, members, regions, deep, points *...  27.9 us
    pallas_call x1, Pallas kernels, local(): pl.pallas_call(finish, out_shape=(jax.ShapeDtypeStruct((own_nodes, width)...  0.68 us

profile of v7, /device:TPU:1, one launch (start us, length us, event | category | flops | bytes accessed | tf_op | source)
XLA Modules:
  0.0 29.2 jit_solution(1659012202486146143)
XLA Ops:
  0.6 27.9 %shard_map.95 = (f32[32,1024]{1,0:T(8,128)S(1)}, f32[8,128]{1,0:T(8,128)S(1)}) custom-call(bf16[32,1024]{1,0:T(8,128)(2,1)} %bitcast.10, bf16[256,1024]{1,0:T(8,128)(2,1)} %bitcast.7, s32[3,256]{1,0:T(4,128)} %bitcast.11, f32[100,256]{1,0:T(8,128)} %bitcast.9, bf16[1024,1024]{1,0:T(8,128)(2,1)} %wq_in.1, bf16[1024,1024]{1,0:T(8,128)(2,1)} %wk_in.1, ...), custom_call_target="tpu_custom_call" | custom-call | tf_op jit(solution)/shard_map/pallas_call | solution.py:424
  28.5 0.7 %shard_map.96 = (f32[32,1024]{1,0:T(8,128)}, f32[1,1]{1,0:T(1,128)}) custom-call(f32[32,1024]{1,0:T(8,128)S(1)} %get-tuple-element.6.grad, f32[8,128]{1,0:T(8,128)S(1)} %get-tuple-element.7.loss), custom_call_target="tpu_custom_call" | custom-call | tf_op jit(solution)/shard_map/pallas_call | solution.py:479
